TPU v7x, 32 devices: a whole 2x2x4 slice. The times are simulated.
32 devices in a mesh: ctx: 16 (over z, y, x), tp: 2 (over core).
Axes of the slice: x: 2, y: 2, z: 4, core: 2. Of those that a mesh axis runs over, the one named last changes fastest.
Arguments:
- outer_input: bfloat16 [1024, 8192], P('ctx', 'tp'), may hold values from -6 to 6
- inner_input: bfloat16 [1024, 8192], P('ctx', 'tp'), may hold values from -6 to 6
- value_input: bfloat16 [1024, 8192], P('ctx', 'tp'), may hold values from -6 to 6
- feature_taps: bfloat16 [3, 7, 8192], P(None, None, 'tp'), may hold values from -2 to 2
- medium_taps: bfloat16 [128, 512], P(None, 'tp'), may hold values from -0.5 to 0.5
- decay_rates: float32 [512, 16], P('tp'), may hold values from 1e-05 to 0.04
- residues: float32 [512, 16], P('tp'), may hold values from -4 to 4
- residual: bfloat16 [1024, 8192], P('ctx', 'tp'), may hold values from -72 to 72
- norm_gain: bfloat16 [8192], P('tp'), may hold values from 0.5 to 1.5
Outputs:
- normed: bfloat16 [1024, 8192], P('ctx', 'tp')
All inputs are finite; a program needn't handle non-finite values.
Results may differ from a plain program's by a relative error of at most 0.0039.
Values may be sent and summed in bfloat16 or wider, within the bound.
A program may use at most 128 MiB of HBM per device.

v0:
```python
import jax
import jax.numpy as jnp
from jax import lax
from jax.sharding import PartitionSpec as P

D = 8192


def passed_along(array, axis, by):
    size = lax.axis_size(axis)
    pairs = [(i, i + by) for i in range(size) if 0 <= i + by < size]
    return lax.ppermute(array, axis, pairs)


def entering(part, axis, combine, identity):
    place = lax.axis_index(axis)
    gathered = jax.tree.map(lambda a: lax.all_gather(a, axis), part)
    state = jax.tree.map(lambda a, e: jnp.zeros_like(a) + jnp.asarray(e, a.dtype), part, identity)

    def one(lap, state):
        return combine(
            state, jax.tree.map(lambda a: lax.dynamic_index_in_dim(a, lap, 0, False), gathered)
        )

    return lax.fori_loop(0, place, one, state)


def banded(reversed_taps, row_count, width):
    group_count, tap_count = reversed_taps.shape
    period = width + 1
    padded = jnp.pad(reversed_taps, ((0, 0), (0, period - tap_count)))
    tiled = jnp.tile(padded, (1, row_count))
    return tiled[:, : row_count * width].reshape(group_count, row_count, width)


def featurize(extended, tap_table, row_count):
    rim_rows = tap_table.shape[0] - 1
    summed = jnp.zeros((row_count, extended.shape[1]), jnp.float32)
    for offset in range(tap_table.shape[0]):
        window = extended[rim_rows - offset : rim_rows - offset + row_count].astype(jnp.float32)
        summed = summed + tap_table[offset].astype(jnp.float32)[None, :] * window
    return summed


def product_rim(product, rim_depth):
    row_count = product.shape[0]
    pieces = []
    for distance in range(1, (rim_depth - 1) // row_count + 2):
        needed = min(row_count, rim_depth - (distance - 1) * row_count)
        arrived = passed_along(product[row_count - needed :], "ctx", distance)
        pieces = [arrived] + pieces
    return jnp.concatenate(pieces, 0)


def combine_modes(earlier, later):
    return (earlier[0] * later[0], earlier[1] * later[0] + later[1])


def on_device(
    outer_input,
    inner_input,
    value_input,
    feature_taps,
    medium_taps,
    decay_rates,
    residues,
    residual,
    norm_gain,
):
    row_count, channels = outer_input.shape
    group_count, mode_count = decay_rates.shape
    group_width = channels // group_count
    feat_rim = feature_taps.shape[1] - 1
    medium_rim = medium_taps.shape[0] - 1
    highest = lax.Precision.HIGHEST
    rim_outer, rim_inner, rim_value = passed_along(
        (
            outer_input[row_count - feat_rim :],
            inner_input[row_count - feat_rim :],
            value_input[row_count - feat_rim :],
        ),
        "ctx",
        1,
    )
    inner_feat = featurize(jnp.concatenate([rim_inner, inner_input], 0), feature_taps[1], row_count)
    value_feat = featurize(jnp.concatenate([rim_value, value_input], 0), feature_taps[2], row_count)
    product = (inner_feat * value_feat).astype(jnp.bfloat16)
    extended = jnp.concatenate([product_rim(product, medium_rim), product], 0)
    outer_feat = featurize(jnp.concatenate([rim_outer, outer_input], 0), feature_taps[0], row_count)
    band_medium = banded(medium_taps[::-1].T, row_count, row_count + medium_rim)
    extended_groups = extended.reshape(row_count + medium_rim, group_count, group_width)
    medium_part = jnp.einsum(
        "gts,sgc->tgc", band_medium, extended_groups, preferred_element_type=jnp.float32
    )
    lag_rows = jnp.arange(row_count, dtype=jnp.float32)[:, None, None]
    mode_weight = residues * jnp.sqrt(2.0 * decay_rates / mode_count)
    powers = jnp.exp(-decay_rates[None] * lag_rows)
    long_taps = jnp.sum(powers * mode_weight[None], axis=2)
    band_long = banded(long_taps[::-1].T, row_count, 2 * row_count - 1)[:, :, row_count - 1 :]
    product_wide = product.reshape(row_count, group_count, group_width).astype(jnp.float32)
    within = jnp.einsum("gts,sgc->tgc", band_long, product_wide, precision=highest)
    to_end = jnp.exp(-decay_rates[None] * (row_count - 1.0 - lag_rows))
    local_state = jnp.einsum("tgc,tgn->gcn", product_wide, to_end, precision=highest)
    block_decay = jnp.exp(-decay_rates * row_count)[:, None, :]
    neutral = (jnp.ones_like(block_decay), jnp.zeros_like(local_state))
    prefix = entering((block_decay, local_state), "ctx", combine_modes, neutral)
    incoming = prefix[1]
    from_start = powers * jnp.exp(-decay_rates)[None]
    carried = jnp.einsum(
        "tgn,gcn->tgc", from_start, incoming * mode_weight[:, None, :], precision=highest
    )
    mixed_conv = (medium_part + within + carried).reshape(row_count, channels)
    hidden = residual.astype(jnp.float32) + outer_feat * mixed_conv
    square_sum = lax.psum(jnp.sum(hidden * hidden, axis=1), "tp")
    normed = (
        hidden * norm_gain.astype(jnp.float32)[None, :] / jnp.sqrt(square_sum / D + 1e-05)[:, None]
    ).astype(jnp.bfloat16)
    return normed


def solution(mesh):
    return jax.shard_map(
        on_device,
        mesh=mesh,
        in_specs=(
            P("ctx", "tp"),
            P("ctx", "tp"),
            P("ctx", "tp"),
            P(None, None, "tp"),
            P(None, "tp"),
            P("tp", None),
            P("tp", None),
            P("ctx", "tp"),
            P("tp"),
        ),
        out_specs=P("ctx", "tp"),
        check_vma=False,
    )
```

profile of v0, /device:TPU:31, one launch (start us, length us, event | category | flops | bytes accessed | tf_op | source)
XLA Modules:
  0.0 226.8 jit_solution(3092466674784826932)
XLA Ops:
  10.9 2.8 %slice_convert_fusion.20 = (f32[1,1,4096]{2,1,0:T(1,128)}, f32[1,1,4096]{2,1,0:T(1,128)S(1)}, f32[1,1,4096]{2,1,0:T(1,128)S(1)}, f32[1,1,4096]{2,1,0:T(1,128)S(1...) fusion(bf16[3,7,4096]{2,1,0:T(8,128)(2,1)} %param.14), kind=kLoop, calls=%fused_computation.87 | loop fusion | flops 77824 | bytes 466944 | tf_op jit(solution)/shard_map/convert_element_type | solution.py:41
  16.7 5.2 %multiply_convert_fusion = bf16[64,4096]{1,0:T(8,128)(2,1)S(1)} fusion(bf16[64,4096]{1,0:T(8,128)(2,1)} %param.13, bf16[64,4096]{1,0:T(8,128)(2,1)} %param.12, bf16[6,4096]{1,0:T(8,128)(2,1)S(1)} %collective-permute-done.2, bf16[6,4096]{1,0:T(8,128)(2,1)S(1)} %collective-permute-done.1, f32[4096]{0:T(1024)S(1)} %bitcast.95, f32[4096]{0:T(1024)S(1)} %bitcast.94, ...), kind=kLoop, calls=%fused_computation.36 | loop fusion | flops 20447232 | bytes 1900544 | tf_op jit(solution)/shard_map/convert_element_type | solution.py:87
  22.7 2.0 fusion.3
  33.9 3.0 %slice.260 = bf16[256,12224]{0,1:T(8,128)(2,1)} slice(bf16[256,12288]{0,1:T(8,128)(2,1)S(1)} %bitcast.63), slice={[0:256], [0:12224]} | slice | bytes 12517376 | tf_op jit(solution)/shard_map/slice | solution.py:33
  36.9 8.5 %reshape.226 = bf16[256,64,191]{0,2,1:T(8,128)(2,1)} reshape(bf16[256,12224]{0,1:T(8,128)(2,1)} %slice.260) | data formatting | bytes 12517376 | tf_op jit(solution)/shard_map/reshape | solution.py:33
  45.4 12.1 %copy.32 = bf16[256,64,191]{2,1,0:T(8,128)(2,1)} copy(bf16[256,64,191]{0,2,1:T(8,128)(2,1)} %reshape.226) | data formatting | bytes 12517376 | tf_op jit(solution)/shard_map/reshape | solution.py:33
  57.5 37.7 %all-gather = f32[4096,16]{0,1:T(8,128)S(1)} all-gather(f32[256,16]{0,1:T(8,128)S(1)} %copy-done.13), channel_id=2, replica_groups=mesh['ctx'=16,'tp'=2] {'ctx'}, dimensions={0}, use_global_device_ids=true | all-gather | bytes 278528 | tf_op jit(solution)/shard_map/all_gather | solution.py:17
  99.9 3.8 %slice.261 = f32[256,8128]{0,1:T(8,128)} slice(f32[256,8192]{0,1:T(8,128)S(1)} %bitcast.62), slice={[0:256], [0:8128]} | slice | bytes 16646144 | tf_op jit(solution)/shard_map/slice | solution.py:33
  103.6 7.3 %reshape.228 = f32[256,64,127]{0,2,1:T(8,128)} reshape(f32[256,8128]{0,1:T(8,128)} %slice.261) | data formatting | bytes 16646144 | tf_op jit(solution)/shard_map/reshape | solution.py:33
  110.9 5.0 %slice.262 = f32[256,64,64]{0,2,1:T(8,128)} slice(f32[256,64,127]{0,2,1:T(8,128)} %reshape.228), slice={[0:256], [0:64], [63:127]} | slice | bytes 8388608 | tf_op jit(solution)/shard_map/slice | solution.py:99
  115.9 9.2 %copy.46 = f32[256,64,64]{2,1,0:T(8,128)} copy(f32[256,64,64]{0,2,1:T(8,128)} %slice.262) | data formatting | bytes 8388608
  127.2 3.1 %copy.31 = bf16[191,4096]{0,1:T(8,128)(2,1)S(1)} copy(bf16[191,4096]{1,0:T(8,128)(2,1)} %pad_maximum_fusion) | data formatting | bytes 3129344 | tf_op jit(solution)/shard_map/concatenate | solution.py:88
  130.4 7.0 %fusion.25 = f32[256,16,64]{2,1,0:T(8,128)} fusion(bf16[191,256,16]{0,2,1:T(8,128)(2,1)S(1)} %bitcast.67, bf16[256,64,191]{2,1,0:T(8,128)(2,1)} %copy.32), kind=kOutput, calls=%fused_computation.91 | convolution fusion | flops 100139008 | bytes 8871936 | tf_op jit(solution)/shard_map/gts,sgc->tgc/dot_general | solution.py:92
  137.4 5.9 %copy.49 = f32[32,8,16,256]{3,2,1,0:T(8,128)} copy(f32[32,8,16,256]{3,1,2,0:T(8,128)} %bitcast.69) | data formatting | bytes 8388608
  143.3 43.8 %while.12 = (s32[]{:T(128)}, f32[256,16,16]{0,2,1:T(8,128)S(1)}, s32[]{:T(128)}, f32[16,256,1,16]{1,0,3,2:T(8,128)}, f32[16,256,16,16]{1,0,3,2:T(8,128)}, /*index=5*/s32[]{:T(128)}, s32[]{:T(128)}, s32[]{:T(128)}) while((s32[]{:T(128)}, f32[256,16,16]{0,2,1:T(8,128)S(1)}, s32[]{:T(128)}, f32[16,256,1,16]{1,0,3,2:T(8,128)}, ...), condition=%wide.region_2.3_spmd, body=%wide.region_1.2_spmd.sunk | while | flops 131077 | bytes 1392767 | solution.py:25
  143.3 1.8 constant_dynamic-slice_fusion.4
  146.2 1.8 constant_dynamic-slice_fusion.4
  149.1 1.8 constant_dynamic-slice_fusion.4
  152.0 1.8 constant_dynamic-slice_fusion.4
  154.9 1.8 constant_dynamic-slice_fusion.4
  157.8 1.8 constant_dynamic-slice_fusion.4
  160.7 1.8 constant_dynamic-slice_fusion.4
  163.6 1.8 constant_dynamic-slice_fusion.4
  175.2 1.8 constant_dynamic-slice_fusion.4
  178.2 1.8 constant_dynamic-slice_fusion.4
  181.1 1.8 constant_dynamic-slice_fusion.4
  184.0 1.8 constant_dynamic-slice_fusion.4
  187.8 2.2 copy.42
  190.0 3.9 %fusion.1 = f32[256,16,64]{2,1,0:T(8,128)S(1)} fusion(f32[256,16,16]{2,1,0:T(8,128)S(1)} %copy.42, f32[256,16]{1,0:T(8,128)} %copy.41, f32[256,16]{1,0:T(8,128)S(1)} %copy.34), kind=kOutput, calls=%fused_computation.5 | convolution fusion | flops 50855936 | bytes 1343488 | tf_op jit(solution)/shard_map/tgn,gcn->tgc/dot_general | solution.py:109
  193.9 9.0 %add_add_fusion = f32[256,16,64]{2,1,0:T(8,128)S(1)} fusion(f32[256,16,64]{2,1,0:T(8,128)S(1)} %fusion.1, f32[256,16,64]{2,1,0:T(8,128)S(1)} %copy-done, bf16[64,256,16]{0,2,1:T(8,128)(2,1)S(1)} %bitcast.65, f32[256,64,64]{2,1,0:T(8,128)} %copy.46), kind=kOutput, calls=%fused_computation.10 | convolution fusion | flops 201850880 | bytes 7864320 | tf_op jit(solution)/shard_map/gts,sgc->tgc/dot_general | solution.py:101
  203.8 4.2 %multiply_reduce_fusion.1 = (f32[64]{0:T(128)S(1)}, f32[64,4096]{1,0:T(8,128)S(1)}) fusion(f32[64,4096]{1,0:T(8,128)S(1)} %copy.43, bf16[64,4096]{1,0:T(8,128)(2,1)} %param.11, bf16[6,4096]{1,0:T(8,128)(2,1)} %collective-permute-done, f32[4096]{0:T(1024)S(1)} %bitcast.76, f32[4096]{0:T(1024)S(1)} %bitcast.77, f32[4096]{0:T(1024)S(1)} %bitcast.78, ...), kind=kLoop, calls=%fused_computation.30 | loop fusion | flops 11272128 | bytes 3309824 | tf_op jit(solution)/shard_map/reduce_sum | solution.py:114
  207.9 11.0 %psum.7 = f32[64]{0:T(128)S(1)} all-reduce(f32[64]{0:T(128)S(1)} %get-tuple-element.75), channel_id=1, replica_groups=mesh['ctx'=16,'tp'=2] {'tp'}, use_global_device_ids=true, to_apply=%region_4.5 | all-reduce | flops 64 | bytes 512 | tf_op jit(solution)/shard_map/psum | solution.py:114
  (121 shorter events, 47.3 us)
Async XLA Ops:
  6.5 130.8 %all-gather.4.cloned.1.call-start = ((), (), s32[]{:S(2)}) async-start(), calls=%async_computation | async-start | bytes 4456448 | tf_op jit(solution)/shard_map/all_gather | solution.py:17
  7.4 9.2 %collective-permute-start.1 = (bf16[6,4096]{1,0:T(8,128)(2,1)S(1)}, bf16[6,4096]{1,0:T(8,128)(2,1)S(1)}, u32[]{:S(2)}, u32[]{:S(2)}) collective-permute-start(bf16[6,4096]{1,0:T(8,128)(2,1)S(1)} %slice.199), channel_id=1, source_target_pairs={{0,2},{2,4},{4,6},{6,8},{8,10},{10,12},{12,14},{14,16},{16,18},{18... | collective-permute-start | bytes 147464 | tf_op jit(solution)/shard_map/ppermute | solution.py:12
  9.6 7.1 %collective-permute-start.2 = (bf16[6,4096]{1,0:T(8,128)(2,1)S(1)}, bf16[6,4096]{1,0:T(8,128)(2,1)S(1)}, u32[]{:S(2)}, u32[]{:S(2)}) collective-permute-start(bf16[6,4096]{1,0:T(8,128)(2,1)S(1)} %slice.213), channel_id=1, source_target_pairs={{0,2},{2,4},{4,6},{6,8},{8,10},{10,12},{12,14},{14,16},{16,18},{18... | collective-permute-start | bytes 147464 | tf_op jit(solution)/shard_map/ppermute | solution.py:12
  16.6 6.0 %copy-start.15 = (f32[64]{0:T(128)S(1)}, f32[64]{0:T(128)}, u32[]{:S(2)}) copy-start(f32[64]{0:T(128)} %iota_subtract_fusion) | copy-start | bytes 772
  21.9 0.8 copy-start.1
  24.7 8.3 %copy-start.11 = (bf16[128,256]{1,0:T(8,128)(2,1)S(1)}, bf16[128,256]{1,0:T(8,128)(2,1)}, u32[]{:S(2)}) copy-start(bf16[128,256]{1,0:T(8,128)(2,1)} %param.15) | copy-start | bytes 196612
  26.5 99.3 %collective-permute-start.4 = (bf16[64,4096]{1,0:T(8,128)(2,1)}, bf16[64,4096]{1,0:T(8,128)(2,1)S(1)}, u32[]{:S(2)}, u32[]{:S(2)}) collective-permute-start(bf16[64,4096]{1,0:T(8,128)(2,1)} %copy-done.1), channel_id=1, source_target_pairs={{0,2},{2,4},{4,6},{6,8},{8,10},{10,12},{12,14},{14,16},{16,18},{18... | collective-permute-start | bytes 1572872 | tf_op jit(solution)/shard_map/ppermute | solution.py:12
  28.9 96.8 %collective-permute-start.3 = (bf16[63,4096]{1,0:T(8,128)(2,1)S(1)}, bf16[63,4096]{1,0:T(8,128)(2,1)S(1)}, u32[]{:S(2)}, u32[]{:S(2)}) collective-permute-start(bf16[63,4096]{1,0:T(8,128)(2,1)S(1)} %slice.259), channel_id=1, source_target_pairs={{0,4},{2,6},{4,8},{6,10},{8,12},{10,14},{12,16},{14,18},{16,20},{1... | collective-permute-start | bytes 1548296 | tf_op jit(solution)/shard_map/ppermute | solution.py:12
  31.7 171.9 %collective-permute-start = (bf16[6,4096]{1,0:T(8,128)(2,1)}, bf16[6,4096]{1,0:T(8,128)(2,1)}, u32[]{:S(2)}, u32[]{:S(2)}) collective-permute-start(bf16[6,4096]{1,0:T(8,128)(2,1)} %slice.185), channel_id=1, source_target_pairs={{0,2},{2,4},{4,6},{6,8},{8,10},{10,12},{12,14},{14,16},{16,18},{18... | collective-permute-start | bytes 147464 | tf_op jit(solution)/shard_map/ppermute | solution.py:12
  45.4 12.1 %copy-start.13 = (f32[256,16]{0,1:T(8,128)S(1)}, f32[256,16]{0,1:T(8,128)}, u32[]{:S(2)}) copy-start(f32[256,16]{0,1:T(8,128)} %get-tuple-element.99) | copy-start | bytes 49156
  45.4 50.6 %copy-start.12 = (f32[256,16]{0,1:T(8,128)S(1)}, f32[256,16]{0,1:T(8,128)}, u32[]{:S(2)}) copy-start(f32[256,16]{0,1:T(8,128)} %get-tuple-element.98) | copy-start | bytes 49156
  115.9 9.3 %copy-start.14 = (bf16[4096]{0:T(1024)(128)(2,1)S(1)}, bf16[4096]{0:T(1024)(128)(2,1)}, u32[]{:S(2)}) copy-start(bf16[4096]{0:T(1024)(128)(2,1)} %param.19) | copy-start | bytes 24580
  115.9 9.9 %copy-start.2 = (bf16[64,4096]{1,0:T(8,128)(2,1)S(1)}, bf16[64,4096]{1,0:T(8,128)(2,1)}, u32[]{:S(2)}) copy-start(bf16[64,4096]{1,0:T(8,128)(2,1)} %copy-done.1) | copy-start | bytes 1572868
  190.0 3.9 %copy-start = (f32[256,16,64]{2,1,0:T(8,128)S(1)}, f32[256,16,64]{2,1,0:T(8,128)}, u32[]{:S(2)}) copy-start(f32[256,16,64]{2,1,0:T(8,128)} %fusion.25) | copy-start | bytes 3145732
  203.0 0.7 copy-start.3
  203.0 0.7 copy-start.4
  203.0 0.7 copy-start.5
  203.0 0.7 copy-start.6
  203.0 0.7 copy-start.7
  203.0 0.8 copy-start.8
  203.0 0.8 copy-start.9
  203.6 15.4 %copy-start.10 = (f32[4096]{0:T(1024)S(1)}, f32[4096]{0:T(1024)}, u32[]{:S(2)}) copy-start(f32[4096]{0:T(1024)} %convert_element_type.355) | copy-start | bytes 49156
Sparse Core Ops, SparseCore 0:
  26.6 99.7 all-gather.3
where the time goes:
time: 229 us; the launch traced here: 227 us
  local copies, waits for them, and re-layouts  113 us (49%)
  blocking collectives  48.7 us (21%)
  other arithmetic  22 us (10%)
  matrix products  21.9 us (10%)
  between operations  13.7 us (6%)
  starting transfers between devices  6.45 us (3%)
    dynamic_slice x45, local copies, waits for them, and re-layouts, one(): lax.dynamic_index_in_dim(a, lap, 0, False)  41.3 us
    all_gather x1, blocking collectives, entering(): gathered = jax.tree.map(lambda a: lax.all_gather(a, axis), part)  37.7 us
    reshape x3, local copies, waits for them, and re-layouts, banded(): return tiled[:, :row_count * width].reshape(group_count, row_count, width)  28 us
    unnamed x36, local copies, waits for them, and re-layouts  16.5 us
    psum x1, blocking collectives, on_device(): square_sum = lax.psum(jnp.sum(hidden * hidden, axis=1), 'tp')  11 us
    dot_general x1, matrix products, on_device(): jnp.einsum('gts,sgc->tgc', band_long, product_wide, precision=highest)  9.03 us
    dot_general x1, matrix products, on_device(): jnp.einsum('gts,sgc->tgc', band_medium, extended_groups, preferred_elemen...  7 us
    slice x2, local copies, waits for them, and re-layouts, banded(): return tiled[:, :row_count * width].reshape(group_count, row_count, width)  6.73 us
  transfers between devices with their start and end apart: 6, of which 0 were waited for; matrix products, arithmetic and copies ran while one was open for 62% of the time, Pallas kernels for 0%

commit v1 on v0

--- a/solution.py
+++ b/solution.py
@@ -1,7 +1,13 @@
+import functools
 import jax
 import jax.numpy as jnp
 from jax import lax
+from jax.experimental import pallas as pl
+from jax.experimental.pallas import tpu as pltpu
 from jax.sharding import PartitionSpec as P
+
+MESH = pl.DeviceIdType.MESH
+BLOCK = 128
 
 D = 8192
 
@@ -56,7 +62,7 @@
     return (earlier[0] * later[0], earlier[1] * later[0] + later[1])
 
 
-def on_device(
+def plain(
     outer_input,
     inner_input,
     value_input,
@@ -118,6 +124,397 @@
     return normed
 
 
+def fused_kernel(
+    n,
+    tpn,
+    outer_ref,
+    inner_ref,
+    value_ref,
+    taps_ref,
+    medium_ref,
+    decay_ref,
+    residues_ref,
+    residual_ref,
+    gain_ref,
+    out_ref,
+    halo_out,
+    halo_in,
+    gate_out,
+    gate_in,
+    ext_a,
+    ext_b,
+    prod_out,
+    prod_all,
+    medium_rev,
+    filt_rev,
+    toep,
+    mixed_out,
+    mixed_in,
+    hidden,
+    sq_out,
+    sq_in,
+    halo_send,
+    halo_recv,
+    prod_send,
+    prod_recv,
+    mixed_send,
+    mixed_recv,
+    sq_send,
+    sq_recv,
+):
+    f32 = jnp.float32
+    me = lax.axis_index("ctx")
+    tp_me = lax.axis_index("tp")
+    rows, channels = outer_ref.shape
+    width = channels // n
+    mode_count = decay_ref.shape[1]
+    group_width = channels // decay_ref.shape[0]
+    group_count = width // group_width
+    tap_count = taps_ref.shape[1]
+    block_count = n * rows // BLOCK
+    per_block = BLOCK // rows
+    tile_groups = 128 // group_width
+    half = channels // 2
+
+    barrier = pltpu.get_barrier_semaphore()
+
+    def greet(k, carry):
+        pl.semaphore_signal(
+            barrier, inc=1, device_id={"ctx": lax.rem(me + k, n)}, device_id_type=MESH
+        )
+        return carry
+
+    lax.fori_loop(1, n, greet, 0)
+    for k in range(1, tpn):
+        pl.semaphore_signal(
+            barrier, inc=1, device_id={"tp": lax.rem(tp_me + k, tpn)}, device_id_type=MESH
+        )
+
+    def last_rows(ref, start, size):
+        return ref[rows - 16 : rows, pl.ds(start, size)].astype(f32)[8:16]
+
+    for start in range(0, channels, 512):
+        halo_out[:, pl.ds(start, 512)] = jnp.concatenate(
+            [last_rows(inner_ref, start, 512), last_rows(value_ref, start, 512)], 0
+        ).astype(jnp.bfloat16)
+    for start in range(0, half, 512):
+        gate_out[:, pl.ds(start, 512)] = jnp.concatenate(
+            [last_rows(outer_ref, start, 512), last_rows(outer_ref, half + start, 512)], 0
+        ).astype(jnp.bfloat16)
+
+    pl.semaphore_wait(barrier, n - 1 + tpn - 1)
+
+    def halo_copy(src, dst, index):
+        return pltpu.make_async_remote_copy(
+            src_ref=src,
+            dst_ref=dst,
+            send_sem=halo_send.at[index],
+            recv_sem=halo_recv.at[index],
+            device_id={"ctx": lax.rem(me + 1, n)},
+            device_id_type=MESH,
+        )
+
+    halo_copies = [halo_copy(halo_out, halo_in, 0), halo_copy(gate_out, gate_in, 1)]
+
+    @pl.when(me < n - 1)
+    def _():
+        for copy in halo_copies:
+            copy.start()
+
+    @pl.when(me == 0)
+    def _():
+        halo_in[...] = jnp.zeros_like(halo_in)
+        gate_in[...] = jnp.zeros_like(gate_in)
+
+    tap_index = lax.broadcasted_iota(jnp.int32, (BLOCK, BLOCK), 0)
+    lane_index = lax.broadcasted_iota(jnp.int32, (BLOCK, BLOCK), 1)
+    for m in range(2):
+        pick = jnp.where(tap_index == BLOCK * m - lane_index, 1.0, 0.0).astype(jnp.bfloat16)
+        medium_rev[m] = lax.dot_general(
+            medium_ref[...], pick, (((0,), (0,)), ((), ())), preferred_element_type=f32
+        )
+    own_groups = pl.ds(pl.multiple_of(me * group_count, group_count), group_count)
+    decay = decay_ref[own_groups, :]
+    weight = residues_ref[own_groups, :] * jnp.sqrt(2.0 * decay / mode_count)
+    lanes = lax.broadcasted_iota(jnp.int32, (group_count, BLOCK), 1)
+    for m in range(block_count + 1):
+        lag = BLOCK * m - lanes
+        lag_rows = jnp.maximum(lag, 0).astype(f32)
+        total = jnp.zeros((group_count, BLOCK), f32)
+        for mode in range(mode_count):
+            total = total + weight[:, mode : mode + 1] * jnp.exp(
+                -decay[:, mode : mode + 1] * lag_rows
+            )
+        total = jnp.where(lag >= 0, total, 0.0)
+        if m < 2:
+            total = total + medium_rev[m, own_groups, :]
+        filt_rev[m] = total
+
+    def featurize(which, ref, rim, ext, start, size):
+        ext[0:8, :] = rim
+        ext[8 : 8 + rows, :] = ref[:, pl.ds(start, size)].astype(f32)
+        taps = taps_ref[which, :, pl.ds(start, size)].astype(f32)
+        summed = taps[0:1] * ext[8 : 8 + rows, :]
+        for offset in range(1, tap_count):
+            summed = summed + taps[offset : offset + 1] * ext[8 - offset : 8 - offset + rows, :]
+        return summed
+
+    def product_for(owner):
+        start = pl.multiple_of(owner * width, width)
+        rim = halo_in[:, pl.ds(start, width)].astype(f32)
+        inner_feat = featurize(1, inner_ref, rim[0:8], ext_a, start, width)
+        value_feat = featurize(2, value_ref, rim[8:16], ext_b, start, width)
+        return (inner_feat * value_feat).astype(jnp.bfloat16)
+
+    def own_rows(place):
+        return pl.ds(pl.multiple_of(place * rows, rows), rows)
+
+    def product_copy(k):
+        return pltpu.make_async_remote_copy(
+            src_ref=prod_out.at[k],
+            dst_ref=prod_all.at[own_rows(me)],
+            send_sem=prod_send.at[k],
+            recv_sem=prod_recv.at[k],
+            device_id={"ctx": lax.rem(me + k, n)},
+            device_id_type=MESH,
+        )
+
+    @pl.when(me > 0)
+    def _():
+        for copy in halo_copies:
+            copy.wait_recv()
+
+    def send_product(k, carry):
+        prod_out[k] = product_for(lax.rem(me + k, n))
+        product_copy(k).start()
+        return carry
+
+    lax.fori_loop(1, n, send_product, 0)
+    prod_all[own_rows(me), :] = product_for(me)
+
+    def gate_chunk(chunk, carry):
+        start = pl.multiple_of(chunk * width, width)
+        low = chunk < n // 2
+        rim_start = pl.multiple_of(lax.rem(chunk, n // 2) * width, width)
+        rim = gate_in[:, pl.ds(rim_start, width)].astype(f32)
+        rim = jnp.where(low, rim[0:8], rim[8:16])
+        hidden[:, pl.ds(start, width)] = featurize(0, outer_ref, rim, ext_a, start, width)
+        return carry
+
+    lax.fori_loop(0, n, gate_chunk, 0)
+
+    def build(g, carry):
+        block_rows = pl.ds(pl.multiple_of(g * BLOCK, BLOCK), BLOCK)
+        upper = lane_index >= tap_index
+        earlier = None
+        for m in range(block_count + 1):
+            row = jnp.broadcast_to(filt_rev[m, pl.ds(g, 1), :], (BLOCK, BLOCK))
+            rolled = pltpu.roll(row, 0, 1, stride=1, stride_axis=0)
+            if m > 0:
+                place = (block_count - m) * BLOCK
+                toep[block_rows, place : place + BLOCK] = jnp.where(
+                    upper, earlier, rolled
+                ).astype(jnp.bfloat16)
+            earlier = rolled
+        return carry
+
+    lax.fori_loop(0, group_count, build, 0)
+
+    def mixed_copy(place):
+        return pltpu.make_async_remote_copy(
+            src_ref=mixed_out.at[place],
+            dst_ref=mixed_in.at[me],
+            send_sem=mixed_send.at[place],
+            recv_sem=mixed_recv.at[lax.rem(place - me + n, n)],
+            device_id={"ctx": place},
+            device_id_type=MESH,
+        )
+
+    lane_group = lax.broadcasted_iota(jnp.int32, (BLOCK, 128), 1) // group_width
+    for block in range(block_count):
+        for place in range(block * per_block, (block + 1) * per_block):
+
+            @pl.when(me != place)
+            def _():
+                pltpu.make_async_remote_copy(
+                    src_ref=prod_out.at[0],
+                    dst_ref=prod_all.at[place * rows : (place + 1) * rows],
+                    send_sem=prod_send.at[0],
+                    recv_sem=prod_recv.at[lax.rem(me - place + n, n)],
+                    device_id={"ctx": place},
+                    device_id_type=MESH,
+                ).wait_recv()
+
+        depth = (block + 1) * BLOCK
+        first = (block_count - 1 - block) * BLOCK
+
+        for tile in range(width // 128):
+            source = prod_all[0:depth, tile * 128 : (tile + 1) * 128]
+            mixed = jnp.zeros((BLOCK, 128), f32)
+            for part in range(0, tile_groups, 4):
+                base = (tile * tile_groups + part) * BLOCK
+                sums = jnp.dot(
+                    toep[base : base + 4 * BLOCK, first:],
+                    source,
+                    preferred_element_type=f32,
+                )
+                for g in range(4):
+                    mixed = jnp.where(
+                        lane_group == part + g, sums[g * BLOCK : (g + 1) * BLOCK], mixed
+                    )
+            mixed = mixed.astype(jnp.bfloat16)
+            for which in range(per_block):
+                mixed_out[block * per_block + which, :, tile * 128 : (tile + 1) * 128] = mixed[
+                    which * rows : (which + 1) * rows
+                ]
+
+        for place in range(block * per_block, (block + 1) * per_block):
+
+            @pl.when(me != place)
+            def _():
+                mixed_copy(place).start()
+
+            @pl.when(me == place)
+            def _():
+                mixed_in[place] = mixed_out[place]
+
+    def gather_hidden(k, square):
+        source = lax.rem(me - k + n, n)
+
+        @pl.when(k > 0)
+        def _():
+            pltpu.make_async_remote_copy(
+                src_ref=mixed_out.at[0],
+                dst_ref=mixed_in.at[source],
+                send_sem=mixed_send.at[0],
+                recv_sem=mixed_recv.at[k],
+                device_id={"ctx": source},
+                device_id_type=MESH,
+            ).wait_recv()
+
+        chunk = pl.ds(pl.multiple_of(source * width, width), width)
+        value = residual_ref[:, chunk].astype(f32) + hidden[:, chunk] * mixed_in[source].astype(f32)
+        hidden[:, chunk] = value
+        for tile in range(width // 128):
+            piece = value[:, tile * 128 : (tile + 1) * 128]
+            square = square + piece * piece
+        return square
+
+    square = lax.fori_loop(0, n, gather_hidden, jnp.zeros((rows, 128), f32))
+    sq_out[...] = square
+
+    def square_copy(k):
+        return pltpu.make_async_remote_copy(
+            src_ref=sq_out,
+            dst_ref=sq_in.at[k],
+            send_sem=sq_send.at[k],
+            recv_sem=sq_recv.at[k],
+            device_id={"tp": lax.rem(tp_me + k, tpn)},
+            device_id_type=MESH,
+        )
+
+    for k in range(1, tpn):
+        square_copy(k).start()
+    for k in range(1, tpn):
+        square_copy(k).wait_recv()
+        square = square + sq_in[k]
+    square_sum = jnp.sum(square, axis=1, keepdims=True)
+    scale = 1.0 / jnp.sqrt(square_sum / (channels * tpn) + 1e-05)
+
+    def finish(chunk, carry):
+        place = pl.ds(pl.multiple_of(chunk * width, width), width)
+        gain = gain_ref[:, place].astype(f32)
+        out_ref[:, place] = (hidden[:, place] * gain * scale).astype(jnp.bfloat16)
+        return carry
+
+    lax.fori_loop(0, n, finish, 0)
+
+    @pl.when(me < n - 1)
+    def _():
+        for copy in halo_copies:
+            copy.wait_send()
+
+    def drain(k, carry):
+        product_copy(k).wait_send()
+        return carry
+
+    lax.fori_loop(1, n, drain, 0)
+
+    def drain_mixed(place, carry):
+        @pl.when(me != place)
+        def _():
+            mixed_copy(place).wait_send()
+
+        return carry
+
+    lax.fori_loop(0, n, drain_mixed, 0)
+    for k in range(1, tpn):
+        square_copy(k).wait_send()
+
+
+def fused(n, tpn, *args):
+    outer_input, inner_input, value_input, taps, medium, decay, residues, residual, gain = args
+    rows, channels = outer_input.shape
+    width = channels // n
+    group_count = decay.shape[0] // n
+    seq = n * rows
+    blocks = seq // BLOCK
+    bf16, f32 = jnp.bfloat16, jnp.float32
+    dma = pltpu.SemaphoreType.DMA
+    return pl.pallas_call(
+        functools.partial(fused_kernel, n, tpn),
+        out_shape=jax.ShapeDtypeStruct((rows, channels), bf16),
+        in_specs=[pl.BlockSpec(memory_space=pltpu.VMEM)] * 9,
+        out_specs=pl.BlockSpec(memory_space=pltpu.VMEM),
+        scratch_shapes=[
+            pltpu.VMEM((16, channels), bf16),
+            pltpu.VMEM((16, channels), bf16),
+            pltpu.VMEM((16, channels // 2), bf16),
+            pltpu.VMEM((16, channels // 2), bf16),
+            pltpu.VMEM((rows + 8, width), f32),
+            pltpu.VMEM((rows + 8, width), f32),
+            pltpu.VMEM((n, rows, width), bf16),
+            pltpu.VMEM((seq, width), bf16),
+            pltpu.VMEM((2, decay.shape[0], BLOCK), f32),
+            pltpu.VMEM((blocks + 1, group_count, BLOCK), f32),
+            pltpu.VMEM((group_count * BLOCK, blocks * BLOCK), bf16),
+            pltpu.VMEM((n, rows, width), bf16),
+            pltpu.VMEM((n, rows, width), bf16),
+            pltpu.VMEM((rows, channels), f32),
+            pltpu.VMEM((rows, 128), f32),
+            pltpu.VMEM((tpn, rows, 128), f32),
+            dma((2,)),
+            dma((2,)),
+            dma((n,)),
+            dma((n,)),
+            dma((n,)),
+            dma((n,)),
+            dma((tpn,)),
+            dma((tpn,)),
+        ],
+        compiler_params=pltpu.CompilerParams(
+            collective_id=0, has_side_effects=True, vmem_limit_bytes=40 * 1024 * 1024
+        ),
+    )(outer_input, inner_input, value_input, taps, medium, decay, residues, residual, gain[None, :])
+
+
+def on_device(*args):
+    n, tpn = lax.axis_size("ctx"), lax.axis_size("tp")
+    rows, channels = args[0].shape
+    medium_rows = args[4].shape[0]
+    groups = args[5].shape[0]
+    fits = (
+        channels % (n * 128) == 0
+        and BLOCK % rows == 0
+        and rows % 16 == 0
+        and groups % (8 * n) == 0
+        and medium_rows == BLOCK
+    )
+    if fits:
+        return fused(n, tpn, *args)
+    return plain(*args)
+
+
 def solution(mesh):
     return jax.shard_map(
         on_device,

time: 229 us -> 46.5 us (0.20)
  local copies, waits for them, and re-layouts: 113 us -> 6.66 us
  blocking collectives: 48.7 us -> 0 us
  Pallas kernels: 0 us -> 39.1 us
  other arithmetic: 22 us -> 0 us
  matrix products: 21.9 us -> 0 us
  between operations: 13.7 us -> 0.05 us
  starting transfers between devices: 6.45 us -> 0 us
    dynamic_slice x45 -> x0, local copies, waits for them, and re-layouts: 41.3 us -> none  [one(): lax.dynamic_index_in_dim(a, lap, 0, False)]
    pallas_call x0 -> x1, Pallas kernels: none -> 39.1 us  [fused(): pl.pallas_call(functools.partial(fused_kernel, n, tpn), out_shape=jax.Sha...]
    all_gather x1 -> x0, blocking collectives: 37.7 us -> none  [entering(): gathered = jax.tree.map(lambda a: lax.all_gather(a, axis), part)]
    reshape x4 -> x0, local copies, waits for them, and re-layouts: 28.5 us -> none  [the longest x3 28 us: banded(): return tiled[:, :row_count * width].reshape(group_count, row_count, width)]
    dot_general x4 -> x0, matrix products: 21.9 us -> none  [the longest x1 9.03 us: on_device(): jnp.einsum('gts,sgc->tgc', band_long, product_wide, precision=highest)]
    slice x7 -> x0, local copies, waits for them, and re-layouts: 16.1 us -> none  [the longest x2 6.73 us: banded(): return tiled[:, :row_count * width].reshape(group_count, row_count, width)]
    psum x1 -> x0, blocking collectives: 11 us -> none  [on_device(): square_sum = lax.psum(jnp.sum(hidden * hidden, axis=1), 'tp')]
    unnamed x36 -> x17, local copies, waits for them, and re-layouts: 16.5 us -> 5.92 us
  transfers between devices with their start and end apart: 6 -> 0, of which waited for: 0 -> 0; matrix products, arithmetic and copies ran while one was open for 62% -> 0% of each run, Pallas kernels for 0% -> 0%
where the time goes in v1:
time: 46.5 us; the launch traced here: 45.8 us
  Pallas kernels  39.1 us (84%)
  local copies, waits for them, and re-layouts  6.66 us (14%)
    pallas_call x1, Pallas kernels, fused(): pl.pallas_call(functools.partial(fused_kernel, n, tpn), out_shape=jax.Sha...  39.1 us
    unnamed x17, local copies, waits for them, and re-layouts  5.92 us

profile of v1, /device:TPU:31, one launch (start us, length us, event | category | flops | bytes accessed | tf_op | source)
XLA Modules:
  0.0 45.8 jit_solution(3840928510530277035)
XLA Ops:
  0.0 0.0 copy-start.6
  0.0 0.0 copy-start.4
  0.0 0.7 %broadcast_in_dim.3.gain_ref = bf16[1,4096]{1,0:T(2,128)(2,1)S(1)} reshape(bf16[4096]{0:T(1024)(128)(2,1)} %param.17) | data formatting | bytes 16384 | tf_op jit(solution)/shard_map/broadcast_in_dim | solution.py:498
  0.8 0.0 copy-done.6
  0.8 0.1 copy.10.decay_ref
  0.9 0.0 copy-start.5
  0.9 0.8 %copy.11.residues_ref = f32[256,16]{1,0:T(8,128)S(1)} copy(f32[256,16]{0,1:T(8,128)} %param.15) | data formatting | bytes 32768 | tf_op args[6]
  1.7 0.0 copy-done.4
  1.7 0.0 copy-done.5
  1.7 0.0 copy-start
  1.8 1.0 %copy-done = bf16[64,4096]{1,0:T(8,128)(2,1)S(1)} copy-done((bf16[64,4096]{1,0:T(8,128)(2,1)S(1)}, bf16[64,4096]{1,0:T(8,128)(2,1)}, u32[]{:S(2)}) %copy-start) | copy-done | bytes 524312
  2.8 0.0 copy-start.1
  2.8 1.0 %copy-done.1 = bf16[64,4096]{1,0:T(8,128)(2,1)S(1)} copy-done((bf16[64,4096]{1,0:T(8,128)(2,1)S(1)}, bf16[64,4096]{1,0:T(8,128)(2,1)}, u32[]{:S(2)}) %copy-start.1) | copy-done | bytes 524312
  3.8 0.0 copy-start.2
  3.8 1.0 %copy-done.2 = bf16[64,4096]{1,0:T(8,128)(2,1)S(1)} copy-done((bf16[64,4096]{1,0:T(8,128)(2,1)S(1)}, bf16[64,4096]{1,0:T(8,128)(2,1)}, u32[]{:S(2)}) %copy-start.2) | copy-done | bytes 524312
  4.9 0.0 copy-start.3
  4.9 1.0 %copy-done.3 = bf16[64,4096]{1,0:T(8,128)(2,1)S(1)} copy-done((bf16[64,4096]{1,0:T(8,128)(2,1)S(1)}, bf16[64,4096]{1,0:T(8,128)(2,1)}, u32[]{:S(2)}) %copy-start.3) | copy-done | bytes 524312
  5.9 39.1 %shard_map.91 = bf16[64,4096]{1,0:T(8,128)(2,1)S(1)} custom-call(bf16[64,4096]{1,0:T(8,128)(2,1)S(1)} %copy-done, bf16[64,4096]{1,0:T(8,128)(2,1)S(1)} %copy-done.1, bf16[64,4096]{1,0:T(8,128)(2,1)S(1)} %copy-done.2, bf16[3,7,4096]{2,1,0:T(8,128)(2,1)S(1)} %copy-done.4, bf16[128,256]{1,0:T(8,128)(2,1)S(1)} %copy-done.5, f32[256,16]{1,0:T(8,128)S(1)} %copy.10.decay_ref, ...), custom_call_target="tpu_custom_call" | custom-call | tf_op jit(solution)/shard_map/pallas_call | solution.py:464
  45.0 0.8 %copy.13 = bf16[64,4096]{1,0:T(8,128)(2,1)} copy(bf16[64,4096]{1,0:T(8,128)(2,1)S(1)} %shard_map.91) | data formatting | bytes 1048576
Async XLA Ops:
  0.0 0.8 %copy-start.6 = (f32[256,16]{0,1:T(8,128)S(1)}, f32[256,16]{0,1:T(8,128)}, u32[]{:S(2)}) copy-start(f32[256,16]{0,1:T(8,128)} %param.14) | copy-start | bytes 49156
  0.0 1.7 %copy-start.4 = (bf16[3,7,4096]{2,1,0:T(8,128)(2,1)S(1)}, bf16[3,7,4096]{2,1,0:T(8,128)(2,1)}, u32[]{:S(2)}) copy-start(bf16[3,7,4096]{2,1,0:T(8,128)(2,1)} %taps_ref.1) | copy-start | bytes 516100
  0.9 0.9 %copy-start.5 = (bf16[128,256]{1,0:T(8,128)(2,1)S(1)}, bf16[128,256]{1,0:T(8,128)(2,1)}, u32[]{:S(2)}) copy-start(bf16[128,256]{1,0:T(8,128)(2,1)} %medium_ref.1) | copy-start | bytes 196612
  1.7 1.0 %copy-start = (bf16[64,4096]{1,0:T(8,128)(2,1)S(1)}, bf16[64,4096]{1,0:T(8,128)(2,1)}, u32[]{:S(2)}) copy-start(bf16[64,4096]{1,0:T(8,128)(2,1)} %outer_ref.1) | copy-start | bytes 1572868
  2.8 1.0 %copy-start.1 = (bf16[64,4096]{1,0:T(8,128)(2,1)S(1)}, bf16[64,4096]{1,0:T(8,128)(2,1)}, u32[]{:S(2)}) copy-start(bf16[64,4096]{1,0:T(8,128)(2,1)} %inner_ref.1) | copy-start | bytes 1572868
  3.8 1.0 %copy-start.2 = (bf16[64,4096]{1,0:T(8,128)(2,1)S(1)}, bf16[64,4096]{1,0:T(8,128)(2,1)}, u32[]{:S(2)}) copy-start(bf16[64,4096]{1,0:T(8,128)(2,1)} %value_ref.1) | copy-start | bytes 1572868
  4.9 1.0 %copy-start.3 = (bf16[64,4096]{1,0:T(8,128)(2,1)S(1)}, bf16[64,4096]{1,0:T(8,128)(2,1)}, u32[]{:S(2)}) copy-start(bf16[64,4096]{1,0:T(8,128)(2,1)} %residual_ref.1) | copy-start | bytes 1572868

commit v2 on v1

--- a/solution.py
+++ b/solution.py
@@ -127,6 +127,16 @@
 def fused_kernel(
     n,
     tpn,
+    outer_hbm,
+    inner_hbm,
+    value_hbm,
+    taps_hbm,
+    medium_hbm,
+    decay_hbm,
+    residues_hbm,
+    residual_hbm,
+    gain_hbm,
+    out_ref,
     outer_ref,
     inner_ref,
     value_ref,
@@ -136,7 +146,8 @@
     residues_ref,
     residual_ref,
     gain_ref,
-    out_ref,
+    decay_rows,
+    weight_rows,
     halo_out,
     halo_in,
     gate_out,
@@ -153,6 +164,7 @@
     hidden,
     sq_out,
     sq_in,
+    load_sem,
     halo_send,
     halo_recv,
     prod_send,
@@ -167,8 +179,8 @@
     tp_me = lax.axis_index("tp")
     rows, channels = outer_ref.shape
     width = channels // n
-    mode_count = decay_ref.shape[1]
-    group_width = channels // decay_ref.shape[0]
+    mode_count = decay_ref.shape[0]
+    group_width = channels // decay_ref.shape[1]
     group_count = width // group_width
     tap_count = taps_ref.shape[1]
     block_count = n * rows // BLOCK
@@ -176,6 +188,25 @@
     tile_groups = 128 // group_width
     half = channels // 2
 
+    loads = [
+        pltpu.make_async_copy(source, target, load_sem.at[index])
+        for index, (source, target) in enumerate(
+            [
+                (inner_hbm, inner_ref),
+                (value_hbm, value_ref),
+                (outer_hbm, outer_ref),
+                (decay_hbm, decay_ref),
+                (residues_hbm, residues_ref),
+                (medium_hbm, medium_ref),
+                (taps_hbm, taps_ref),
+                (residual_hbm, residual_ref),
+                (gain_hbm, gain_ref),
+            ]
+        )
+    ]
+    for load in loads:
+        load.start()
+
     barrier = pltpu.get_barrier_semaphore()
 
     def greet(k, carry):
@@ -193,6 +224,8 @@
     def last_rows(ref, start, size):
         return ref[rows - 16 : rows, pl.ds(start, size)].astype(f32)[8:16]
 
+    for load in loads[:3]:
+        load.wait()
     for start in range(0, channels, 512):
         halo_out[:, pl.ds(start, 512)] = jnp.concatenate(
             [last_rows(inner_ref, start, 512), last_rows(value_ref, start, 512)], 0
@@ -226,6 +259,9 @@
         halo_in[...] = jnp.zeros_like(halo_in)
         gate_in[...] = jnp.zeros_like(gate_in)
 
+    for load in loads[3:6]:
+        load.wait()
+
     tap_index = lax.broadcasted_iota(jnp.int32, (BLOCK, BLOCK), 0)
     lane_index = lax.broadcasted_iota(jnp.int32, (BLOCK, BLOCK), 1)
     for m in range(2):
@@ -234,8 +270,10 @@
             medium_ref[...], pick, (((0,), (0,)), ((), ())), preferred_element_type=f32
         )
     own_groups = pl.ds(pl.multiple_of(me * group_count, group_count), group_count)
-    decay = decay_ref[own_groups, :]
-    weight = residues_ref[own_groups, :] * jnp.sqrt(2.0 * decay / mode_count)
+    decay_rows[...] = decay_ref[...].T
+    weight_rows[...] = (residues_ref[...] * jnp.sqrt(2.0 * decay_ref[...] / mode_count)).T
+    decay = decay_rows[own_groups, :]
+    weight = weight_rows[own_groups, :]
     lanes = lax.broadcasted_iota(jnp.int32, (group_count, BLOCK), 1)
     for m in range(block_count + 1):
         lag = BLOCK * m - lanes
@@ -250,59 +288,6 @@
             total = total + medium_rev[m, own_groups, :]
         filt_rev[m] = total
 
-    def featurize(which, ref, rim, ext, start, size):
-        ext[0:8, :] = rim
-        ext[8 : 8 + rows, :] = ref[:, pl.ds(start, size)].astype(f32)
-        taps = taps_ref[which, :, pl.ds(start, size)].astype(f32)
-        summed = taps[0:1] * ext[8 : 8 + rows, :]
-        for offset in range(1, tap_count):
-            summed = summed + taps[offset : offset + 1] * ext[8 - offset : 8 - offset + rows, :]
-        return summed
-
-    def product_for(owner):
-        start = pl.multiple_of(owner * width, width)
-        rim = halo_in[:, pl.ds(start, width)].astype(f32)
-        inner_feat = featurize(1, inner_ref, rim[0:8], ext_a, start, width)
-        value_feat = featurize(2, value_ref, rim[8:16], ext_b, start, width)
-        return (inner_feat * value_feat).astype(jnp.bfloat16)
-
-    def own_rows(place):
-        return pl.ds(pl.multiple_of(place * rows, rows), rows)
-
-    def product_copy(k):
-        return pltpu.make_async_remote_copy(
-            src_ref=prod_out.at[k],
-            dst_ref=prod_all.at[own_rows(me)],
-            send_sem=prod_send.at[k],
-            recv_sem=prod_recv.at[k],
-            device_id={"ctx": lax.rem(me + k, n)},
-            device_id_type=MESH,
-        )
-
-    @pl.when(me > 0)
-    def _():
-        for copy in halo_copies:
-            copy.wait_recv()
-
-    def send_product(k, carry):
-        prod_out[k] = product_for(lax.rem(me + k, n))
-        product_copy(k).start()
-        return carry
-
-    lax.fori_loop(1, n, send_product, 0)
-    prod_all[own_rows(me), :] = product_for(me)
-
-    def gate_chunk(chunk, carry):
-        start = pl.multiple_of(chunk * width, width)
-        low = chunk < n // 2
-        rim_start = pl.multiple_of(lax.rem(chunk, n // 2) * width, width)
-        rim = gate_in[:, pl.ds(rim_start, width)].astype(f32)
-        rim = jnp.where(low, rim[0:8], rim[8:16])
-        hidden[:, pl.ds(start, width)] = featurize(0, outer_ref, rim, ext_a, start, width)
-        return carry
-
-    lax.fori_loop(0, n, gate_chunk, 0)
-
     def build(g, carry):
         block_rows = pl.ds(pl.multiple_of(g * BLOCK, BLOCK), BLOCK)
         upper = lane_index >= tap_index
@@ -319,6 +304,62 @@
         return carry
 
     lax.fori_loop(0, group_count, build, 0)
+
+    for load in loads[6:]:
+        load.wait()
+
+    def featurize(which, ref, rim, ext, start, size):
+        ext[0:8, :] = rim
+        ext[8 : 8 + rows, :] = ref[:, pl.ds(start, size)].astype(f32)
+        taps = taps_ref[which, :, pl.ds(start, size)].astype(f32)
+        summed = taps[0:1] * ext[8 : 8 + rows, :]
+        for offset in range(1, tap_count):
+            summed = summed + taps[offset : offset + 1] * ext[8 - offset : 8 - offset + rows, :]
+        return summed
+
+    def product_for(owner):
+        start = pl.multiple_of(owner * width, width)
+        rim = halo_in[:, pl.ds(start, width)].astype(f32)
+        inner_feat = featurize(1, inner_ref, rim[0:8], ext_a, start, width)
+        value_feat = featurize(2, value_ref, rim[8:16], ext_b, start, width)
+        return (inner_feat * value_feat).astype(jnp.bfloat16)
+
+    def own_rows(place):
+        return pl.ds(pl.multiple_of(place * rows, rows), rows)
+
+    def product_copy(k):
+        return pltpu.make_async_remote_copy(
+            src_ref=prod_out.at[k],
+            dst_ref=prod_all.at[own_rows(me)],
+            send_sem=prod_send.at[k],
+            recv_sem=prod_recv.at[k],
+            device_id={"ctx": lax.rem(me + k, n)},
+            device_id_type=MESH,
+        )
+
+    @pl.when(me > 0)
+    def _():
+        for copy in halo_copies:
+            copy.wait_recv()
+
+    def send_product(k, carry):
+        prod_out[k] = product_for(lax.rem(me + k, n))
+        product_copy(k).start()
+        return carry
+
+    lax.fori_loop(1, n, send_product, 0)
+    prod_all[own_rows(me), :] = product_for(me)
+
+    def gate_chunk(chunk, carry):
+        start = pl.multiple_of(chunk * width, width)
+        low = chunk < n // 2
+        rim_start = pl.multiple_of(lax.rem(chunk, n // 2) * width, width)
+        rim = gate_in[:, pl.ds(rim_start, width)].astype(f32)
+        rim = jnp.where(low, rim[0:8], rim[8:16])
+        hidden[:, pl.ds(start, width)] = featurize(0, outer_ref, rim, ext_a, start, width)
+        return carry
+
+    lax.fori_loop(0, n, gate_chunk, 0)
 
     def mixed_copy(place):
         return pltpu.make_async_remote_copy(
@@ -422,8 +463,9 @@
     scale = 1.0 / jnp.sqrt(square_sum / (channels * tpn) + 1e-05)
 
     def finish(chunk, carry):
-        place = pl.ds(pl.multiple_of(chunk * width, width), width)
-        gain = gain_ref[:, place].astype(f32)
+        start = pl.multiple_of(chunk * width, width)
+        gain = gain_ref[pl.ds(start, width)].astype(f32).reshape(1, width)
+        place = pl.ds(start, width)
         out_ref[:, place] = (hidden[:, place] * gain * scale).astype(jnp.bfloat16)
         return carry
 
@@ -456,7 +498,8 @@
     outer_input, inner_input, value_input, taps, medium, decay, residues, residual, gain = args
     rows, channels = outer_input.shape
     width = channels // n
-    group_count = decay.shape[0] // n
+    all_groups, mode_count = decay.shape
+    group_count = all_groups // n
     seq = n * rows
     blocks = seq // BLOCK
     bf16, f32 = jnp.bfloat16, jnp.float32
@@ -464,9 +507,20 @@
     return pl.pallas_call(
         functools.partial(fused_kernel, n, tpn),
         out_shape=jax.ShapeDtypeStruct((rows, channels), bf16),
-        in_specs=[pl.BlockSpec(memory_space=pltpu.VMEM)] * 9,
+        in_specs=[pl.BlockSpec(memory_space=pltpu.HBM)] * 9,
         out_specs=pl.BlockSpec(memory_space=pltpu.VMEM),
         scratch_shapes=[
+            pltpu.VMEM((rows, channels), bf16),
+            pltpu.VMEM((rows, channels), bf16),
+            pltpu.VMEM((rows, channels), bf16),
+            pltpu.VMEM(taps.shape, bf16),
+            pltpu.VMEM(medium.shape, bf16),
+            pltpu.VMEM((mode_count, all_groups), f32),
+            pltpu.VMEM((mode_count, all_groups), f32),
+            pltpu.VMEM((rows, channels), bf16),
+            pltpu.VMEM(gain.shape, bf16),
+            pltpu.VMEM((all_groups, mode_count), f32),
+            pltpu.VMEM((all_groups, mode_count), f32),
             pltpu.VMEM((16, channels), bf16),
             pltpu.VMEM((16, channels), bf16),
             pltpu.VMEM((16, channels // 2), bf16),
@@ -483,6 +537,7 @@
             pltpu.VMEM((rows, channels), f32),
             pltpu.VMEM((rows, 128), f32),
             pltpu.VMEM((tpn, rows, 128), f32),
+            dma((9,)),
             dma((2,)),
             dma((2,)),
             dma((n,)),
@@ -493,9 +548,9 @@
             dma((tpn,)),
         ],
         compiler_params=pltpu.CompilerParams(
-            collective_id=0, has_side_effects=True, vmem_limit_bytes=40 * 1024 * 1024
+            collective_id=0, has_side_effects=True, vmem_limit_bytes=63 * 1024 * 1024
         ),
-    )(outer_input, inner_input, value_input, taps, medium, decay, residues, residual, gain[None, :])
+    )(outer_input, inner_input, value_input, taps, medium, decay.T, residues.T, residual, gain)
 
 
 def on_device(*args):

time: 46.5 us -> 42.7 us (0.918)
  local copies, waits for them, and re-layouts: 6.66 us -> 1.87 us
  Pallas kernels: 39.1 us -> 40.1 us
    unnamed x17 -> x1, local copies, waits for them, and re-layouts: 5.92 us -> 1.87 us
    pallas_call x1, Pallas kernels: 39.1 us -> 40.1 us  [fused(): pl.pallas_call(functools.partial(fused_kernel, n, tpn), out_shape=jax.Sha...]
    broadcast_in_dim x1 -> x0, local copies, waits for them, and re-layouts: 0.75 us -> none  [fused(): gain[None, :]]
where the time goes in v2:
time: 42.7 us; the launch traced here: 42 us
  Pallas kernels  40.1 us (94%)
  local copies, waits for them, and re-layouts  1.87 us (4%)
    pallas_call x1, Pallas kernels, fused(): pl.pallas_call(functools.partial(fused_kernel, n, tpn), out_shape=jax.Sha...  40.1 us
    unnamed x1, local copies, waits for them, and re-layouts  1.87 us

profile of v2, /device:TPU:31, one launch (start us, length us, event | category | flops | bytes accessed | tf_op | source)
XLA Modules:
  0.0 42.0 jit_solution(6626610242679955167)
XLA Ops:
  0.0 40.1 %shard_map.91 = bf16[64,4096]{1,0:T(8,128)(2,1)} custom-call(bf16[64,4096]{1,0:T(8,128)(2,1)} %outer_hbm.1, bf16[64,4096]{1,0:T(8,128)(2,1)} %inner_hbm.1, bf16[64,4096]{1,0:T(8,128)(2,1)} %value_hbm.1, bf16[3,7,4096]{2,1,0:T(8,128)(2,1)} %taps_hbm.1, bf16[128,256]{1,0:T(8,128)(2,1)} %medium_hbm.1, f32[16,256]{1,0:T(8,128)} %bitcast.2, f32[16,256]{1,0:T(8,128)} %bitcast.3, ...), custom_call_target="tpu_custom_call" | custom-call | tf_op jit(solution)/shard_map/pallas_call | solution.py:507
  40.2 1.9 %copy.11 = bf16[64,4096]{1,0:T(8,128)(2,1)} copy(bf16[64,4096]{1,0:T(8,128)(2,1)} %shard_map.91) | data formatting | bytes 1048576

commit v3 on v2

--- a/solution.py
+++ b/solution.py
@@ -125,6 +125,7 @@
 
 
 def fused_kernel(
+    part,
     n,
     tpn,
     outer_hbm,
@@ -159,6 +160,15 @@
     medium_rev,
     filt_rev,
     toep,
+    decay_wide,
+    weight_wide,
+    carry_taps,
+    carry_rows,
+    state_taps,
+    state_out,
+    state_in,
+    rim_in,
+    mixed_sum,
     mixed_out,
     mixed_in,
     hidden,
@@ -171,22 +181,30 @@
     prod_recv,
     mixed_send,
     mixed_recv,
+    link_send,
+    link_recv,
     sq_send,
     sq_recv,
 ):
-    f32 = jnp.float32
+    f32, bf16 = jnp.float32, jnp.bfloat16
     me = lax.axis_index("ctx")
     tp_me = lax.axis_index("tp")
+    parts = n // part
+    mine = me // part
+    spot = lax.rem(me, part)
     rows, channels = outer_ref.shape
-    width = channels // n
-    mode_count = decay_ref.shape[0]
-    group_width = channels // decay_ref.shape[1]
+    width = channels // part
+    mode_count, all_groups = decay_ref.shape
+    group_width = channels // all_groups
     group_count = width // group_width
     tap_count = taps_ref.shape[1]
-    block_count = n * rows // BLOCK
-    per_block = BLOCK // rows
+    tokens = part * rows
+    block_count = tokens // BLOCK
+    pair_count = block_count // 2
     tile_groups = 128 // group_width
+    tile_count = width // 128
     half = channels // 2
+    step = min(width, 256)
 
     loads = [
         pltpu.make_async_copy(source, target, load_sem.at[index])
@@ -195,10 +213,10 @@
                 (inner_hbm, inner_ref),
                 (value_hbm, value_ref),
                 (outer_hbm, outer_ref),
+                (taps_hbm, taps_ref),
                 (decay_hbm, decay_ref),
                 (residues_hbm, residues_ref),
                 (medium_hbm, medium_ref),
-                (taps_hbm, taps_ref),
                 (residual_hbm, residual_ref),
                 (gain_hbm, gain_ref),
             ]
@@ -207,19 +225,27 @@
     for load in loads:
         load.start()
 
+    def peer(k):
+        return {"ctx": mine * part + lax.rem(spot + k, part)}
+
     barrier = pltpu.get_barrier_semaphore()
 
-    def greet(k, carry):
-        pl.semaphore_signal(
-            barrier, inc=1, device_id={"ctx": lax.rem(me + k, n)}, device_id_type=MESH
-        )
-        return carry
-
-    lax.fori_loop(1, n, greet, 0)
+    def signal(device):
+        pl.semaphore_signal(barrier, inc=1, device_id=device, device_id_type=MESH)
+
+    for k in range(1, part):
+        signal(peer(k))
     for k in range(1, tpn):
-        pl.semaphore_signal(
-            barrier, inc=1, device_id={"tp": lax.rem(tp_me + k, tpn)}, device_id_type=MESH
-        )
+        signal({"tp": lax.rem(tp_me + k, tpn)})
+    if parts > 1:
+
+        @pl.when(mine > 0)
+        def _():
+            signal({"ctx": lax.rem(me - part + n, n)})
+
+            @pl.when(spot == 0)
+            def _():
+                signal({"ctx": lax.rem(me - 1 + n, n)})
 
     def last_rows(ref, start, size):
         return ref[rows - 16 : rows, pl.ds(start, size)].astype(f32)[8:16]
@@ -229,13 +255,16 @@
     for start in range(0, channels, 512):
         halo_out[:, pl.ds(start, 512)] = jnp.concatenate(
             [last_rows(inner_ref, start, 512), last_rows(value_ref, start, 512)], 0
-        ).astype(jnp.bfloat16)
+        ).astype(bf16)
     for start in range(0, half, 512):
         gate_out[:, pl.ds(start, 512)] = jnp.concatenate(
             [last_rows(outer_ref, start, 512), last_rows(outer_ref, half + start, 512)], 0
-        ).astype(jnp.bfloat16)
-
-    pl.semaphore_wait(barrier, n - 1 + tpn - 1)
+        ).astype(bf16)
+
+    awaited = part - 1 + tpn - 1
+    if parts > 1:
+        awaited = awaited + (1 - mine // (parts - 1)) * (1 + (spot + 1) // part)
+    pl.semaphore_wait(barrier, awaited)
 
     def halo_copy(src, dst, index):
         return pltpu.make_async_remote_copy(
@@ -251,25 +280,91 @@
 
     @pl.when(me < n - 1)
     def _():
-        for copy in halo_copies:
-            copy.start()
+        halo_copies[0].start()
+        halo_copies[1].start()
 
     @pl.when(me == 0)
     def _():
         halo_in[...] = jnp.zeros_like(halo_in)
         gate_in[...] = jnp.zeros_like(gate_in)
 
-    for load in loads[3:6]:
+    loads[3].wait()
+
+    def windows(which, ext, start, size, first, count):
+        taps = taps_ref[which, :, pl.ds(start, size)].astype(f32)
+        summed = taps[0:1] * ext[first : first + count, :]
+        for offset in range(1, tap_count):
+            summed = summed + taps[offset : offset + 1] * ext[
+                first - offset : first - offset + count, :
+            ]
+        return summed
+
+    per_spot = width // step
+
+    def lower_product(chunk, carry):
+        start = pl.multiple_of(chunk * step, step)
+        inside = pl.ds(pl.multiple_of(lax.rem(chunk, per_spot) * step, step), step)
+        ext_a[8 : 8 + rows, :] = inner_ref[:, pl.ds(start, step)].astype(f32)
+        ext_b[8 : 8 + rows, :] = value_ref[:, pl.ds(start, step)].astype(f32)
+        inner_feat = windows(1, ext_a, start, step, 24, rows - 16)
+        value_feat = windows(2, ext_b, start, step, 24, rows - 16)
+        prod_out[chunk // per_spot, 16:rows, inside] = (inner_feat * value_feat).astype(bf16)
+        return carry
+
+    lax.fori_loop(0, channels // step, lower_product, 0)
+
+    @pl.when(me > 0)
+    def _():
+        halo_copies[0].wait_recv()
+
+    def upper_product(owner):
+        for piece in range(per_spot):
+            start = pl.multiple_of(owner * width + piece * step, step)
+            rim = halo_in[:, pl.ds(start, step)].astype(f32)
+            ext_a[0:8, :] = rim[0:8]
+            ext_b[0:8, :] = rim[8:16]
+            ext_a[8:24, :] = inner_ref[0:16, pl.ds(start, step)].astype(f32)
+            ext_b[8:24, :] = value_ref[0:16, pl.ds(start, step)].astype(f32)
+            inner_feat = windows(1, ext_a, start, step, 8, 16)
+            value_feat = windows(2, ext_b, start, step, 8, 16)
+            prod_out[owner, 0:16, piece * step : (piece + 1) * step] = (
+                inner_feat * value_feat
+            ).astype(bf16)
+
+    def own_rows(place):
+        return pl.ds(pl.multiple_of(BLOCK + place * rows, rows), rows)
+
+    def product_copy(k):
+        return pltpu.make_async_remote_copy(
+            src_ref=prod_out.at[lax.rem(spot + k, part)],
+            dst_ref=prod_all.at[own_rows(spot)],
+            send_sem=prod_send.at[k],
+            recv_sem=prod_recv.at[k],
+            device_id=peer(k),
+            device_id_type=MESH,
+        )
+
+    def send_product(k, carry):
+        upper_product(lax.rem(spot + k, part))
+        product_copy(k).start()
+        return carry
+
+    lax.fori_loop(1, part, send_product, 0)
+    upper_product(spot)
+    prod_all[own_rows(spot), :] = prod_out[spot]
+    prod_all[0:BLOCK, :] = jnp.zeros((BLOCK, width), bf16)
+
+    for load in loads[4:7]:
         load.wait()
 
     tap_index = lax.broadcasted_iota(jnp.int32, (BLOCK, BLOCK), 0)
     lane_index = lax.broadcasted_iota(jnp.int32, (BLOCK, BLOCK), 1)
     for m in range(2):
-        pick = jnp.where(tap_index == BLOCK * m - lane_index, 1.0, 0.0).astype(jnp.bfloat16)
+        pick = jnp.where(tap_index == BLOCK * m - lane_index, 1.0, 0.0).astype(bf16)
         medium_rev[m] = lax.dot_general(
             medium_ref[...], pick, (((0,), (0,)), ((), ())), preferred_element_type=f32
         )
-    own_groups = pl.ds(pl.multiple_of(me * group_count, group_count), group_count)
+    own_groups = pl.ds(pl.multiple_of(spot * group_count, group_count), group_count)
     decay_rows[...] = decay_ref[...].T
     weight_rows[...] = (residues_ref[...] * jnp.sqrt(2.0 * decay_ref[...] / mode_count)).T
     decay = decay_rows[own_groups, :]
@@ -288,9 +383,47 @@
             total = total + medium_rev[m, own_groups, :]
         filt_rev[m] = total
 
+    blank = jnp.zeros((group_count, 128 - 3 * mode_count), f32)
+    decay_wide[...] = jnp.concatenate([decay, decay, decay, blank], 1)
+    weight_wide[...] = jnp.concatenate([weight, weight, weight, blank], 1)
+
+    mode_row = lax.broadcasted_iota(jnp.int32, (mode_count, 128), 0)
+    mode_lane = lax.broadcasted_iota(jnp.int32, (mode_count, 128), 1)
+
+    def decay_column(g):
+        row = jnp.broadcast_to(decay_wide[pl.ds(g, 1), :], (mode_count, 128))
+        return jnp.sum(jnp.where(mode_row == mode_lane, row, 0.0), axis=1, keepdims=True)
+
+    def channel_decay(tile):
+        spread = jnp.zeros((mode_count, 128), f32)
+        for g in range(tile_groups):
+            spread = jnp.where(
+                mode_lane // group_width == g, decay_column(tile * tile_groups + g), spread
+            )
+        return spread
+
+    if parts > 1:
+
+        @pl.when(mine < parts - 1)
+        def _():
+            left = (
+                tokens - 1 - lax.broadcasted_iota(jnp.int32, (mode_count, tokens), 1)
+            ).astype(f32)
+
+            def decays(g, carry):
+                place = pl.ds(pl.multiple_of(g * mode_count, mode_count), mode_count)
+                value = jnp.exp(-decay_column(g) * left)
+                high = value.astype(bf16)
+                state_taps[0, place, :] = high
+                state_taps[1, place, :] = (value - high.astype(f32)).astype(bf16)
+                return carry
+
+            lax.fori_loop(0, group_count, decays, 0)
+
+    upper = lane_index >= tap_index
+
     def build(g, carry):
         block_rows = pl.ds(pl.multiple_of(g * BLOCK, BLOCK), BLOCK)
-        upper = lane_index >= tap_index
         earlier = None
         for m in range(block_count + 1):
             row = jnp.broadcast_to(filt_rev[m, pl.ds(g, 1), :], (BLOCK, BLOCK))
@@ -299,128 +432,238 @@
                 place = (block_count - m) * BLOCK
                 toep[block_rows, place : place + BLOCK] = jnp.where(
                     upper, earlier, rolled
-                ).astype(jnp.bfloat16)
+                ).astype(bf16)
             earlier = rolled
         return carry
 
     lax.fori_loop(0, group_count, build, 0)
 
-    for load in loads[6:]:
-        load.wait()
-
-    def featurize(which, ref, rim, ext, start, size):
-        ext[0:8, :] = rim
-        ext[8 : 8 + rows, :] = ref[:, pl.ds(start, size)].astype(f32)
-        taps = taps_ref[which, :, pl.ds(start, size)].astype(f32)
-        summed = taps[0:1] * ext[8 : 8 + rows, :]
-        for offset in range(1, tap_count):
-            summed = summed + taps[offset : offset + 1] * ext[8 - offset : 8 - offset + rows, :]
-        return summed
-
-    def product_for(owner):
-        start = pl.multiple_of(owner * width, width)
-        rim = halo_in[:, pl.ds(start, width)].astype(f32)
-        inner_feat = featurize(1, inner_ref, rim[0:8], ext_a, start, width)
-        value_feat = featurize(2, value_ref, rim[8:16], ext_b, start, width)
-        return (inner_feat * value_feat).astype(jnp.bfloat16)
-
-    def own_rows(place):
-        return pl.ds(pl.multiple_of(place * rows, rows), rows)
-
-    def product_copy(k):
+    if parts > 1:
+
+        @pl.when(mine > 0)
+        def _():
+            carry_rows[...] = jnp.zeros_like(carry_rows)
+            ahead = (tap_index + 1).astype(f32)
+
+            def build_carry(g, carry):
+                block_rows = pl.ds(pl.multiple_of(g * BLOCK, BLOCK), BLOCK)
+                value = weight_wide[pl.ds(g, 1), :] * jnp.exp(-decay_wide[pl.ds(g, 1), :] * ahead)
+                high = value.astype(bf16).astype(f32)
+                carry_taps[block_rows, 0:BLOCK] = jnp.where(
+                    lane_index < 2 * mode_count, high, value - high
+                ).astype(bf16)
+                row = medium_rev[1, pl.ds(spot * group_count + g, 1), :]
+                rolled = pltpu.roll(
+                    jnp.broadcast_to(row, (BLOCK, BLOCK)), 0, 1, stride=1, stride_axis=0
+                )
+                carry_taps[block_rows, BLOCK : 2 * BLOCK] = jnp.where(upper, rolled, 0.0).astype(
+                    bf16
+                )
+                return carry
+
+            lax.fori_loop(0, group_count, build_carry, 0)
+
+    @pl.when(me > 0)
+    def _():
+        halo_copies[1].wait_recv()
+
+    def gate_chunk(chunk, carry):
+        start = pl.multiple_of(chunk * step, step)
+        low = start < half
+        rim_start = pl.multiple_of(lax.rem(start, half), step)
+        rim = gate_in[:, pl.ds(rim_start, step)].astype(f32)
+        ext_a[0:8, :] = jnp.where(low, rim[0:8], rim[8:16])
+        ext_a[8 : 8 + rows, :] = outer_ref[:, pl.ds(start, step)].astype(f32)
+        hidden[:, pl.ds(start, step)] = windows(0, ext_a, start, step, 8, rows)
+        return carry
+
+    lax.fori_loop(0, channels // step, gate_chunk, 0)
+
+    def wait_product(place):
+        @pl.when(spot != place)
+        def _():
+            pltpu.make_async_remote_copy(
+                src_ref=prod_out.at[0],
+                dst_ref=prod_all.at[BLOCK + place * rows : BLOCK + (place + 1) * rows],
+                send_sem=prod_send.at[0],
+                recv_sem=prod_recv.at[lax.rem(spot - place + part, part)],
+                device_id=peer(1),
+                device_id_type=MESH,
+            ).wait_recv()
+
+    def link_copy(src, dst, index):
         return pltpu.make_async_remote_copy(
-            src_ref=prod_out.at[k],
-            dst_ref=prod_all.at[own_rows(me)],
-            send_sem=prod_send.at[k],
-            recv_sem=prod_recv.at[k],
-            device_id={"ctx": lax.rem(me + k, n)},
+            src_ref=src,
+            dst_ref=dst,
+            send_sem=link_send.at[index],
+            recv_sem=link_recv.at[index],
+            device_id={"ctx": lax.rem(me + part, n)},
             device_id_type=MESH,
         )
 
-    @pl.when(me > 0)
-    def _():
-        for copy in halo_copies:
-            copy.wait_recv()
-
-    def send_product(k, carry):
-        prod_out[k] = product_for(lax.rem(me + k, n))
-        product_copy(k).start()
+    rim_copy = link_copy(prod_all.at[tokens : tokens + BLOCK], rim_in, 0)
+    state_copy = link_copy(state_out, state_in, 1)
+    last_spots = range(part - BLOCK // rows, part)
+    for place in last_spots:
+        wait_product(place)
+    if parts > 1:
+
+        @pl.when(mine < parts - 1)
+        def _():
+            rim_copy.start()
+
+    for place in range(part - BLOCK // rows):
+        wait_product(place)
+
+    if parts > 1:
+
+        @pl.when(mine < parts - 1)
+        def _():
+            tile_rows = tile_groups * mode_count
+            if parts > 2:
+
+                @pl.when(mine > 0)
+                def _():
+                    state_copy.wait_recv()
+
+            for tile in range(tile_count):
+                place = slice(tile * 128, (tile + 1) * 128)
+                source = prod_all[BLOCK : BLOCK + tokens, place]
+                taps_rows = slice(tile * tile_rows, (tile + 1) * tile_rows)
+                sums = jnp.dot(
+                    state_taps[0, taps_rows, :], source, preferred_element_type=f32
+                ) + jnp.dot(state_taps[1, taps_rows, :], source, preferred_element_type=f32)
+                state = jnp.zeros((mode_count, 128), f32)
+                for g in range(tile_groups):
+                    state = jnp.where(
+                        mode_lane // group_width == g,
+                        sums[g * mode_count : (g + 1) * mode_count],
+                        state,
+                    )
+                state_out[:, place] = state
+            if parts > 2:
+
+                @pl.when(mine > 0)
+                def _():
+                    for tile in range(tile_count):
+                        place = slice(tile * 128, (tile + 1) * 128)
+                        state_out[:, place] = state_out[:, place] + state_in[:, place] * jnp.exp(
+                            -channel_decay(tile) * tokens
+                        )
+
+            state_copy.start()
+
+    lane_group = lax.broadcasted_iota(jnp.int32, (BLOCK, 128), 1) // group_width
+
+    def grouped(taps, columns, source, base):
+        sums = [jnp.zeros((BLOCK, 128), f32)] * 2
+        for first in range(0, tile_groups, 4):
+            start = pl.multiple_of(base + first * BLOCK, BLOCK)
+            result = jnp.dot(
+                taps[pl.ds(start, 4 * BLOCK), columns], source, preferred_element_type=f32
+            )
+            for g in range(4):
+                for side in range(2):
+                    sums[side] = jnp.where(
+                        lane_group == first + g,
+                        result[g * BLOCK : (g + 1) * BLOCK, side * 128 : (side + 1) * 128],
+                        sums[side],
+                    )
+        return sums
+
+    def own_part(tile, carry):
+        place = pl.ds(pl.multiple_of(tile * 128, 128), 128)
+        base = tile * tile_groups * BLOCK
+        for pair in range(pair_count):
+            depth = (pair + 1) * 2 * BLOCK
+            columns = slice(block_count * BLOCK - depth, block_count * BLOCK)
+            source = jnp.concatenate(
+                [prod_all[0:depth, place], prod_all[BLOCK : BLOCK + depth, place]], 1
+            )
+            sums = grouped(toep, columns, source, base)
+            for side in range(2):
+                at = (pair * 2 + side) * BLOCK
+                mixed_sum[at : at + BLOCK, place] = sums[side]
         return carry
 
-    lax.fori_loop(1, n, send_product, 0)
-    prod_all[own_rows(me), :] = product_for(me)
-
-    def gate_chunk(chunk, carry):
-        start = pl.multiple_of(chunk * width, width)
-        low = chunk < n // 2
-        rim_start = pl.multiple_of(lax.rem(chunk, n // 2) * width, width)
-        rim = gate_in[:, pl.ds(rim_start, width)].astype(f32)
-        rim = jnp.where(low, rim[0:8], rim[8:16])
-        hidden[:, pl.ds(start, width)] = featurize(0, outer_ref, rim, ext_a, start, width)
-        return carry
-
-    lax.fori_loop(0, n, gate_chunk, 0)
+    lax.fori_loop(0, tile_count, own_part, 0)
 
     def mixed_copy(place):
         return pltpu.make_async_remote_copy(
             src_ref=mixed_out.at[place],
-            dst_ref=mixed_in.at[me],
+            dst_ref=mixed_in.at[spot],
             send_sem=mixed_send.at[place],
-            recv_sem=mixed_recv.at[lax.rem(place - me + n, n)],
-            device_id={"ctx": place},
+            recv_sem=mixed_recv.at[lax.rem(place - spot + part, part)],
+            device_id={"ctx": mine * part + place},
             device_id_type=MESH,
         )
 
-    lane_group = lax.broadcasted_iota(jnp.int32, (BLOCK, 128), 1) // group_width
-    for block in range(block_count):
-        for place in range(block * per_block, (block + 1) * per_block):
-
-            @pl.when(me != place)
+    if parts > 1:
+
+        @pl.when(mine > 0)
+        def _():
+            rim_copy.wait_recv()
+            if parts > 2:
+
+                @pl.when(mine == parts - 1)
+                def _():
+                    state_copy.wait_recv()
+
+            else:
+                state_copy.wait_recv()
+
+            for tile in range(tile_count):
+                place = slice(tile * 128, (tile + 1) * 128)
+                fade = channel_decay(tile)
+                carry_rows[0, BLOCK : 2 * BLOCK, tile * 256 : tile * 256 + 128] = rim_in[:, place]
+                for block in range(block_count):
+                    state = state_in[:, place] * jnp.exp(-fade * (block * BLOCK))
+                    high = state.astype(bf16)
+                    low = (state - high.astype(f32)).astype(bf16)
+                    at = tile * 256 + block % 2 * 128
+                    carry_rows[block // 2, 0 : 3 * mode_count, at : at + 128] = jnp.concatenate(
+                        [high, low, high], 0
+                    )
+
+    pair_spots = 2 * BLOCK // rows
+    for pair in range(pair_count):
+        if parts > 1:
+
+            @pl.when(mine > 0)
             def _():
-                pltpu.make_async_remote_copy(
-                    src_ref=prod_out.at[0],
-                    dst_ref=prod_all.at[place * rows : (place + 1) * rows],
-                    send_sem=prod_send.at[0],
-                    recv_sem=prod_recv.at[lax.rem(me - place + n, n)],
-                    device_id={"ctx": place},
-                    device_id_type=MESH,
-                ).wait_recv()
-
-        depth = (block + 1) * BLOCK
-        first = (block_count - 1 - block) * BLOCK
-
-        for tile in range(width // 128):
-            source = prod_all[0:depth, tile * 128 : (tile + 1) * 128]
-            mixed = jnp.zeros((BLOCK, 128), f32)
-            for part in range(0, tile_groups, 4):
-                base = (tile * tile_groups + part) * BLOCK
-                sums = jnp.dot(
-                    toep[base : base + 4 * BLOCK, first:],
-                    source,
-                    preferred_element_type=f32,
-                )
-                for g in range(4):
-                    mixed = jnp.where(
-                        lane_group == part + g, sums[g * BLOCK : (g + 1) * BLOCK], mixed
+                depth = 2 * BLOCK if pair == 0 else BLOCK
+
+                def carried(tile, carry):
+                    place = pl.ds(pl.multiple_of(tile * 128, 128), 128)
+                    source = carry_rows[
+                        pair, 0:depth, pl.ds(pl.multiple_of(tile * 256, 256), 256)
+                    ]
+                    sums = grouped(
+                        carry_taps, slice(0, depth), source, tile * tile_groups * BLOCK
                     )
-            mixed = mixed.astype(jnp.bfloat16)
-            for which in range(per_block):
-                mixed_out[block * per_block + which, :, tile * 128 : (tile + 1) * 128] = mixed[
-                    which * rows : (which + 1) * rows
-                ]
-
-        for place in range(block * per_block, (block + 1) * per_block):
-
-            @pl.when(me != place)
+                    for side in range(2):
+                        at = (pair * 2 + side) * BLOCK
+                        mixed_sum[at : at + BLOCK, place] += sums[side]
+                    return carry
+
+                lax.fori_loop(0, tile_count, carried, 0)
+
+        for place in range(pair * pair_spots, (pair + 1) * pair_spots):
+            mixed_out[place] = mixed_sum[place * rows : (place + 1) * rows, :].astype(bf16)
+
+            @pl.when(spot != place)
             def _():
                 mixed_copy(place).start()
 
-            @pl.when(me == place)
+            @pl.when(spot == place)
             def _():
                 mixed_in[place] = mixed_out[place]
 
+    loads[7].wait()
+    loads[8].wait()
+
     def gather_hidden(k, square):
-        source = lax.rem(me - k + n, n)
+        source = lax.rem(spot - k + part, part)
 
         @pl.when(k > 0)
         def _():
@@ -429,19 +672,23 @@
                 dst_ref=mixed_in.at[source],
                 send_sem=mixed_send.at[0],
                 recv_sem=mixed_recv.at[k],
-                device_id={"ctx": source},
+                device_id=peer(1),
                 device_id_type=MESH,
             ).wait_recv()
 
-        chunk = pl.ds(pl.multiple_of(source * width, width), width)
-        value = residual_ref[:, chunk].astype(f32) + hidden[:, chunk] * mixed_in[source].astype(f32)
-        hidden[:, chunk] = value
-        for tile in range(width // 128):
-            piece = value[:, tile * 128 : (tile + 1) * 128]
-            square = square + piece * piece
+        for piece in range(per_spot):
+            inside = slice(piece * step, (piece + 1) * step)
+            chunk = pl.ds(pl.multiple_of(source * width + piece * step, step), step)
+            value = residual_ref[:, chunk].astype(f32) + hidden[:, chunk] * mixed_in[
+                source, :, inside
+            ].astype(f32)
+            hidden[:, chunk] = value
+            for tile in range(step // 128):
+                cut = value[:, tile * 128 : (tile + 1) * 128]
+                square = square + cut * cut
         return square
 
-    square = lax.fori_loop(0, n, gather_hidden, jnp.zeros((rows, 128), f32))
+    square = lax.fori_loop(0, part, gather_hidden, jnp.zeros((rows, 128), f32))
     sq_out[...] = square
 
     def square_copy(k):
@@ -463,49 +710,51 @@
     scale = 1.0 / jnp.sqrt(square_sum / (channels * tpn) + 1e-05)
 
     def finish(chunk, carry):
-        start = pl.multiple_of(chunk * width, width)
-        gain = gain_ref[pl.ds(start, width)].astype(f32).reshape(1, width)
-        place = pl.ds(start, width)
-        out_ref[:, place] = (hidden[:, place] * gain * scale).astype(jnp.bfloat16)
+        start = pl.multiple_of(chunk * 256, 256)
+        gain = gain_ref[pl.ds(start, 256)].astype(f32).reshape(1, 256)
+        place = pl.ds(start, 256)
+        out_ref[:, place] = (hidden[:, place] * gain * scale).astype(bf16)
         return carry
 
-    lax.fori_loop(0, n, finish, 0)
+    lax.fori_loop(0, channels // 256, finish, 0)
 
     @pl.when(me < n - 1)
     def _():
         for copy in halo_copies:
             copy.wait_send()
 
-    def drain(k, carry):
+    if parts > 1:
+
+        @pl.when(mine < parts - 1)
+        def _():
+            rim_copy.wait_send()
+            state_copy.wait_send()
+
+    for k in range(1, part):
         product_copy(k).wait_send()
-        return carry
-
-    lax.fori_loop(1, n, drain, 0)
-
-    def drain_mixed(place, carry):
-        @pl.when(me != place)
+    for place in range(part):
+
+        @pl.when(spot != place)
         def _():
             mixed_copy(place).wait_send()
 
-        return carry
-
-    lax.fori_loop(0, n, drain_mixed, 0)
     for k in range(1, tpn):
         square_copy(k).wait_send()
 
 
-def fused(n, tpn, *args):
+def fused(part, n, tpn, *args):
     outer_input, inner_input, value_input, taps, medium, decay, residues, residual, gain = args
     rows, channels = outer_input.shape
-    width = channels // n
+    width = channels // part
     all_groups, mode_count = decay.shape
-    group_count = all_groups // n
-    seq = n * rows
-    blocks = seq // BLOCK
+    group_count = all_groups // part
+    tokens = part * rows
+    blocks = tokens // BLOCK
+    step = min(width, 256)
     bf16, f32 = jnp.bfloat16, jnp.float32
     dma = pltpu.SemaphoreType.DMA
     return pl.pallas_call(
-        functools.partial(fused_kernel, n, tpn),
+        functools.partial(fused_kernel, part, n, tpn),
         out_shape=jax.ShapeDtypeStruct((rows, channels), bf16),
         in_specs=[pl.BlockSpec(memory_space=pltpu.HBM)] * 9,
         out_specs=pl.BlockSpec(memory_space=pltpu.VMEM),
@@ -525,25 +774,36 @@
             pltpu.VMEM((16, channels), bf16),
             pltpu.VMEM((16, channels // 2), bf16),
             pltpu.VMEM((16, channels // 2), bf16),
-            pltpu.VMEM((rows + 8, width), f32),
-            pltpu.VMEM((rows + 8, width), f32),
-            pltpu.VMEM((n, rows, width), bf16),
-            pltpu.VMEM((seq, width), bf16),
-            pltpu.VMEM((2, decay.shape[0], BLOCK), f32),
+            pltpu.VMEM((rows + 8, step), f32),
+            pltpu.VMEM((rows + 8, step), f32),
+            pltpu.VMEM((part, rows, width), bf16),
+            pltpu.VMEM((BLOCK + tokens, width), bf16),
+            pltpu.VMEM((2, all_groups, BLOCK), f32),
             pltpu.VMEM((blocks + 1, group_count, BLOCK), f32),
-            pltpu.VMEM((group_count * BLOCK, blocks * BLOCK), bf16),
-            pltpu.VMEM((n, rows, width), bf16),
-            pltpu.VMEM((n, rows, width), bf16),
+            pltpu.VMEM((group_count * BLOCK, tokens), bf16),
+            pltpu.VMEM((group_count, 128), f32),
+            pltpu.VMEM((group_count, 128), f32),
+            pltpu.VMEM((group_count * BLOCK, 2 * BLOCK), bf16),
+            pltpu.VMEM((blocks // 2, 2 * BLOCK, 2 * width), bf16),
+            pltpu.VMEM((2, group_count * mode_count, tokens), bf16),
+            pltpu.VMEM((mode_count, width), f32),
+            pltpu.VMEM((mode_count, width), f32),
+            pltpu.VMEM((BLOCK, width), bf16),
+            pltpu.VMEM((tokens, width), f32),
+            pltpu.VMEM((part, rows, width), bf16),
+            pltpu.VMEM((part, rows, width), bf16),
             pltpu.VMEM((rows, channels), f32),
             pltpu.VMEM((rows, 128), f32),
             pltpu.VMEM((tpn, rows, 128), f32),
             dma((9,)),
             dma((2,)),
             dma((2,)),
-            dma((n,)),
-            dma((n,)),
-            dma((n,)),
-            dma((n,)),
+            dma((part,)),
+            dma((part,)),
+            dma((part,)),
+            dma((part,)),
+            dma((2,)),
+            dma((2,)),
             dma((tpn,)),
             dma((tpn,)),
         ],
@@ -553,20 +813,31 @@
     )(outer_input, inner_input, value_input, taps, medium, decay.T, residues.T, residual, gain)
 
 
+PART = 8
+
+
 def on_device(*args):
     n, tpn = lax.axis_size("ctx"), lax.axis_size("tp")
     rows, channels = args[0].shape
-    medium_rows = args[4].shape[0]
-    groups = args[5].shape[0]
+    taps_rows, medium_rows = args[3].shape[1], args[4].shape[0]
+    groups, modes = args[5].shape
     fits = (
-        channels % (n * 128) == 0
+        n % PART == 0
+        and channels % (PART * 128) == 0
+        and channels % 1024 == 0
         and BLOCK % rows == 0
-        and rows % 16 == 0
-        and groups % (8 * n) == 0
+        and rows % 32 == 0
+        and (PART * rows) % (2 * BLOCK) == 0
+        and groups % (8 * PART) == 0
+        and 128 % (channels // groups) == 0
+        and channels // groups <= 32
+        and modes % 16 == 0
+        and modes <= 32
+        and taps_rows <= 9
         and medium_rows == BLOCK
     )
     if fits:
-        return fused(n, tpn, *args)
+        return fused(PART, n, tpn, *args)
     return plain(*args)
 
 

time: 42.7 us -> 37.6 us (0.88)
  the two profiles are of different devices: /device:TPU:31 before, /device:TPU:23 now
where the time goes in v3:
time: 37.6 us; the launch traced here: 37.4 us
  Pallas kernels  35.5 us (94%)
  local copies, waits for them, and re-layouts  1.87 us (5%)
    pallas_call x1, Pallas kernels, fused(): pl.pallas_call(functools.partial(fused_kernel, part, n, tpn), out_shape=j...  35.5 us
    unnamed x1, local copies, waits for them, and re-layouts  1.87 us

profile of v3, /device:TPU:23, one launch (start us, length us, event | category | flops | bytes accessed | tf_op | source)
XLA Modules:
  0.0 37.4 jit_solution(12564630545111121163)
XLA Ops:
  0.0 35.5 %shard_map.91 = bf16[64,4096]{1,0:T(8,128)(2,1)} custom-call(bf16[64,4096]{1,0:T(8,128)(2,1)} %outer_hbm.1, bf16[64,4096]{1,0:T(8,128)(2,1)} %inner_hbm.1, bf16[64,4096]{1,0:T(8,128)(2,1)} %value_hbm.1, bf16[3,7,4096]{2,1,0:T(8,128)(2,1)} %taps_hbm.1, bf16[128,256]{1,0:T(8,128)(2,1)} %medium_hbm.1, f32[16,256]{1,0:T(8,128)} %bitcast.2, f32[16,256]{1,0:T(8,128)} %bitcast.3, ...), custom_call_target="tpu_custom_call" | custom-call | tf_op jit(solution)/shard_map/pallas_call | solution.py:756
  35.5 1.9 %copy.11 = bf16[64,4096]{1,0:T(8,128)(2,1)} copy(bf16[64,4096]{1,0:T(8,128)(2,1)} %shard_map.91) | data formatting | bytes 1048576

commit v4 on v3

--- a/solution.py
+++ b/solution.py
@@ -204,7 +204,7 @@
     tile_groups = 128 // group_width
     tile_count = width // 128
     half = channels // 2
-    step = min(width, 256)
+    step = 128
 
     loads = [
         pltpu.make_async_copy(source, target, load_sem.at[index])
@@ -420,49 +420,6 @@
 
             lax.fori_loop(0, group_count, decays, 0)
 
-    upper = lane_index >= tap_index
-
-    def build(g, carry):
-        block_rows = pl.ds(pl.multiple_of(g * BLOCK, BLOCK), BLOCK)
-        earlier = None
-        for m in range(block_count + 1):
-            row = jnp.broadcast_to(filt_rev[m, pl.ds(g, 1), :], (BLOCK, BLOCK))
-            rolled = pltpu.roll(row, 0, 1, stride=1, stride_axis=0)
-            if m > 0:
-                place = (block_count - m) * BLOCK
-                toep[block_rows, place : place + BLOCK] = jnp.where(
-                    upper, earlier, rolled
-                ).astype(bf16)
-            earlier = rolled
-        return carry
-
-    lax.fori_loop(0, group_count, build, 0)
-
-    if parts > 1:
-
-        @pl.when(mine > 0)
-        def _():
-            carry_rows[...] = jnp.zeros_like(carry_rows)
-            ahead = (tap_index + 1).astype(f32)
-
-            def build_carry(g, carry):
-                block_rows = pl.ds(pl.multiple_of(g * BLOCK, BLOCK), BLOCK)
-                value = weight_wide[pl.ds(g, 1), :] * jnp.exp(-decay_wide[pl.ds(g, 1), :] * ahead)
-                high = value.astype(bf16).astype(f32)
-                carry_taps[block_rows, 0:BLOCK] = jnp.where(
-                    lane_index < 2 * mode_count, high, value - high
-                ).astype(bf16)
-                row = medium_rev[1, pl.ds(spot * group_count + g, 1), :]
-                rolled = pltpu.roll(
-                    jnp.broadcast_to(row, (BLOCK, BLOCK)), 0, 1, stride=1, stride_axis=0
-                )
-                carry_taps[block_rows, BLOCK : 2 * BLOCK] = jnp.where(upper, rolled, 0.0).astype(
-                    bf16
-                )
-                return carry
-
-            lax.fori_loop(0, group_count, build_carry, 0)
-
     @pl.when(me > 0)
     def _():
         halo_copies[1].wait_recv()
@@ -503,29 +460,18 @@
 
     rim_copy = link_copy(prod_all.at[tokens : tokens + BLOCK], rim_in, 0)
     state_copy = link_copy(state_out, state_in, 1)
-    last_spots = range(part - BLOCK // rows, part)
-    for place in last_spots:
-        wait_product(place)
+    rim_spots = part - BLOCK // rows
+
     if parts > 1:
 
         @pl.when(mine < parts - 1)
         def _():
+            for place in range(rim_spots, part):
+                wait_product(place)
             rim_copy.start()
-
-    for place in range(part - BLOCK // rows):
-        wait_product(place)
-
-    if parts > 1:
-
-        @pl.when(mine < parts - 1)
-        def _():
+            for place in range(rim_spots):
+                wait_product(place)
             tile_rows = tile_groups * mode_count
-            if parts > 2:
-
-                @pl.when(mine > 0)
-                def _():
-                    state_copy.wait_recv()
-
             for tile in range(tile_count):
                 place = slice(tile * 128, (tile + 1) * 128)
                 source = prod_all[BLOCK : BLOCK + tokens, place]
@@ -545,6 +491,7 @@
 
                 @pl.when(mine > 0)
                 def _():
+                    state_copy.wait_recv()
                     for tile in range(tile_count):
                         place = slice(tile * 128, (tile + 1) * 128)
                         state_out[:, place] = state_out[:, place] + state_in[:, place] * jnp.exp(
@@ -552,6 +499,54 @@
                         )
 
             state_copy.start()
+
+    upper = lane_index >= tap_index
+
+    def build(g, carry):
+        block_rows = pl.ds(pl.multiple_of(g * BLOCK, BLOCK), BLOCK)
+        earlier = None
+        for m in range(block_count + 1):
+            row = jnp.broadcast_to(filt_rev[m, pl.ds(g, 1), :], (BLOCK, BLOCK))
+            rolled = pltpu.roll(row, 0, 1, stride=1, stride_axis=0)
+            if m > 0:
+                place = (block_count - m) * BLOCK
+                toep[block_rows, place : place + BLOCK] = jnp.where(
+                    upper, earlier, rolled
+                ).astype(bf16)
+            earlier = rolled
+        return carry
+
+    lax.fori_loop(0, group_count, build, 0)
+
+    if parts > 1:
+
+        @pl.when(mine > 0)
+        def _():
+            carry_rows[...] = jnp.zeros_like(carry_rows)
+            ahead = (tap_index + 1).astype(f32)
+
+            def build_carry(g, carry):
+                block_rows = pl.ds(pl.multiple_of(g * BLOCK, BLOCK), BLOCK)
+                value = weight_wide[pl.ds(g, 1), :] * jnp.exp(-decay_wide[pl.ds(g, 1), :] * ahead)
+                high = value.astype(bf16).astype(f32)
+                carry_taps[block_rows, 0:BLOCK] = jnp.where(
+                    lane_index < 2 * mode_count, high, value - high
+                ).astype(bf16)
+                row = medium_rev[1, pl.ds(spot * group_count + g, 1), :]
+                rolled = pltpu.roll(
+                    jnp.broadcast_to(row, (BLOCK, BLOCK)), 0, 1, stride=1, stride_axis=0
+                )
+                carry_taps[block_rows, BLOCK : 2 * BLOCK] = jnp.where(upper, rolled, 0.0).astype(
+                    bf16
+                )
+                return carry
+
+            lax.fori_loop(0, group_count, build_carry, 0)
+
+    @pl.when(mine == parts - 1)
+    def _():
+        for place in range(part):
+            wait_product(place)
 
     lane_group = lax.broadcasted_iota(jnp.int32, (BLOCK, 128), 1) // group_width
 
@@ -750,7 +745,7 @@
     group_count = all_groups // part
     tokens = part * rows
     blocks = tokens // BLOCK
-    step = min(width, 256)
+    step = 128
     bf16, f32 = jnp.bfloat16, jnp.float32
     dma = pltpu.SemaphoreType.DMA
     return pl.pallas_call(
@@ -808,7 +803,7 @@
             dma((tpn,)),
         ],
         compiler_params=pltpu.CompilerParams(
-            collective_id=0, has_side_effects=True, vmem_limit_bytes=63 * 1024 * 1024
+            collective_id=0, has_side_effects=True, vmem_limit_bytes=54200 * 1024
         ),
     )(outer_input, inner_input, value_input, taps, medium, decay.T, residues.T, residual, gain)
 

time: 37.6 us -> 38.5 us (1.024)
  local copies, waits for them, and re-layouts: 1.87 us -> 4.69 us
  Pallas kernels: 35.5 us -> 33.4 us
    unnamed x1 -> x11, local copies, waits for them, and re-layouts: 1.87 us -> 4.69 us
    pallas_call x1, Pallas kernels: 35.5 us -> 33.4 us  [fused(): pl.pallas_call(functools.partial(fused_kernel, part, n, tpn), out_shape=j...]
where the time goes in v4:
time: 38.5 us; the launch traced here: 38.1 us
  Pallas kernels  33.4 us (87%)
  local copies, waits for them, and re-layouts  4.69 us (12%)
    pallas_call x1, Pallas kernels, fused(): pl.pallas_call(functools.partial(fused_kernel, part, n, tpn), out_shape=j...  33.4 us
    unnamed x11, local copies, waits for them, and re-layouts  4.69 us

profile of v4, /device:TPU:23, one launch (start us, length us, event | category | flops | bytes accessed | tf_op | source)
XLA Modules:
  0.0 38.1 jit_solution(7868743271398576278)
XLA Ops:
  0.0 0.0 copy-start
  0.0 0.9 %copy-done = bf16[3,7,4096]{2,1,0:T(8,128)(2,1)S(1)} copy-done((bf16[3,7,4096]{2,1,0:T(8,128)(2,1)S(1)}, bf16[3,7,4096]{2,1,0:T(8,128)(2,1)}, u32[]{:S(2)}) %copy-start) | copy-done | bytes 172056
  0.9 0.0 copy-start.1
  0.9 0.8 %copy-done.1 = bf16[128,256]{1,0:T(8,128)(2,1)S(1)} copy-done((bf16[128,256]{1,0:T(8,128)(2,1)S(1)}, bf16[128,256]{1,0:T(8,128)(2,1)}, u32[]{:S(2)}) %copy-start.1) | copy-done | bytes 65560
  1.8 0.0 copy-start.2
  1.8 0.7 %copy-done.2 = f32[256,16]{0,1:T(8,128)S(1)} copy-done((f32[256,16]{0,1:T(8,128)S(1)}, f32[256,16]{0,1:T(8,128)}, u32[]{:S(2)}) %copy-start.2) | copy-done | bytes 16408
  2.5 0.0 copy-start.3
  2.5 0.7 %copy-done.3 = f32[256,16]{0,1:T(8,128)S(1)} copy-done((f32[256,16]{0,1:T(8,128)S(1)}, f32[256,16]{0,1:T(8,128)}, u32[]{:S(2)}) %copy-start.3) | copy-done | bytes 16408
  3.2 0.0 copy-start.4
  3.2 0.7 %copy-done.4 = bf16[4096]{0:T(1024)(128)(2,1)S(1)} copy-done((bf16[4096]{0:T(1024)(128)(2,1)S(1)}, bf16[4096]{0:T(1024)(128)(2,1)}, u32[]{:S(2)}) %copy-start.4) | copy-done | bytes 8216
  3.9 33.4 %shard_map.91 = bf16[64,4096]{1,0:T(8,128)(2,1)S(1)} custom-call(bf16[64,4096]{1,0:T(8,128)(2,1)} %outer_hbm.1, bf16[64,4096]{1,0:T(8,128)(2,1)} %inner_hbm.1, bf16[64,4096]{1,0:T(8,128)(2,1)} %value_hbm.1, bf16[3,7,4096]{2,1,0:T(8,128)(2,1)S(1)} %copy-done, bf16[128,256]{1,0:T(8,128)(2,1)S(1)} %copy-done.1, f32[16,256]{1,0:T(8,128)S(1)} %bitcast.2, ...), custom_call_target="tpu_custom_call" | custom-call | tf_op jit(solution)/shard_map/pallas_call | solution.py:751
  37.3 0.8 %copy.11 = bf16[64,4096]{1,0:T(8,128)(2,1)} copy(bf16[64,4096]{1,0:T(8,128)(2,1)S(1)} %shard_map.91) | data formatting | bytes 1048576
Async XLA Ops:
  0.0 0.9 %copy-start = (bf16[3,7,4096]{2,1,0:T(8,128)(2,1)S(1)}, bf16[3,7,4096]{2,1,0:T(8,128)(2,1)}, u32[]{:S(2)}) copy-start(bf16[3,7,4096]{2,1,0:T(8,128)(2,1)} %taps_hbm.1) | copy-start | bytes 516100
  0.9 0.8 %copy-start.1 = (bf16[128,256]{1,0:T(8,128)(2,1)S(1)}, bf16[128,256]{1,0:T(8,128)(2,1)}, u32[]{:S(2)}) copy-start(bf16[128,256]{1,0:T(8,128)(2,1)} %medium_hbm.1) | copy-start | bytes 196612
  1.8 0.7 %copy-start.2 = (f32[256,16]{0,1:T(8,128)S(1)}, f32[256,16]{0,1:T(8,128)}, u32[]{:S(2)}) copy-start(f32[256,16]{0,1:T(8,128)} %param.14) | copy-start | bytes 49156
  2.5 0.7 %copy-start.3 = (f32[256,16]{0,1:T(8,128)S(1)}, f32[256,16]{0,1:T(8,128)}, u32[]{:S(2)}) copy-start(f32[256,16]{0,1:T(8,128)} %param.15) | copy-start | bytes 49156
  3.2 0.7 %copy-start.4 = (bf16[4096]{0:T(1024)(128)(2,1)S(1)}, bf16[4096]{0:T(1024)(128)(2,1)}, u32[]{:S(2)}) copy-start(bf16[4096]{0:T(1024)(128)(2,1)} %gain_hbm.1) | copy-start | bytes 24580

commit v5 on v4

--- a/solution.py
+++ b/solution.py
@@ -137,6 +137,7 @@
     residues_hbm,
     residual_hbm,
     gain_hbm,
+    out_hbm,
     out_ref,
     outer_ref,
     inner_ref,
@@ -175,6 +176,7 @@
     sq_out,
     sq_in,
     load_sem,
+    store_sem,
     halo_send,
     halo_recv,
     prod_send,
@@ -311,7 +313,7 @@
         prod_out[chunk // per_spot, 16:rows, inside] = (inner_feat * value_feat).astype(bf16)
         return carry
 
-    lax.fori_loop(0, channels // step, lower_product, 0)
+    lax.fori_loop(0, channels // step, lower_product, 0, unroll=4)
 
     @pl.when(me > 0)
     def _():
@@ -434,7 +436,7 @@
         hidden[:, pl.ds(start, step)] = windows(0, ext_a, start, step, 8, rows)
         return carry
 
-    lax.fori_loop(0, channels // step, gate_chunk, 0)
+    lax.fori_loop(0, channels // step, gate_chunk, 0, unroll=4)
 
     def wait_product(place):
         @pl.when(spot != place)
@@ -516,7 +518,7 @@
             earlier = rolled
         return carry
 
-    lax.fori_loop(0, group_count, build, 0)
+    lax.fori_loop(0, group_count, build, 0, unroll=2)
 
     if parts > 1:
 
@@ -541,7 +543,7 @@
                 )
                 return carry
 
-            lax.fori_loop(0, group_count, build_carry, 0)
+            lax.fori_loop(0, group_count, build_carry, 0, unroll=2)
 
     @pl.when(mine == parts - 1)
     def _():
@@ -566,23 +568,6 @@
                     )
         return sums
 
-    def own_part(tile, carry):
-        place = pl.ds(pl.multiple_of(tile * 128, 128), 128)
-        base = tile * tile_groups * BLOCK
-        for pair in range(pair_count):
-            depth = (pair + 1) * 2 * BLOCK
-            columns = slice(block_count * BLOCK - depth, block_count * BLOCK)
-            source = jnp.concatenate(
-                [prod_all[0:depth, place], prod_all[BLOCK : BLOCK + depth, place]], 1
-            )
-            sums = grouped(toep, columns, source, base)
-            for side in range(2):
-                at = (pair * 2 + side) * BLOCK
-                mixed_sum[at : at + BLOCK, place] = sums[side]
-        return carry
-
-    lax.fori_loop(0, tile_count, own_part, 0)
-
     def mixed_copy(place):
         return pltpu.make_async_remote_copy(
             src_ref=mixed_out.at[place],
@@ -593,48 +578,63 @@
             device_id_type=MESH,
         )
 
-    if parts > 1:
-
-        @pl.when(mine > 0)
-        def _():
-            rim_copy.wait_recv()
-            if parts > 2:
-
-                @pl.when(mine == parts - 1)
-                def _():
-                    state_copy.wait_recv()
-
-            else:
+    def take_carry():
+        rim_copy.wait_recv()
+        if parts > 2:
+
+            @pl.when(mine == parts - 1)
+            def _():
                 state_copy.wait_recv()
 
-            for tile in range(tile_count):
-                place = slice(tile * 128, (tile + 1) * 128)
-                fade = channel_decay(tile)
-                carry_rows[0, BLOCK : 2 * BLOCK, tile * 256 : tile * 256 + 128] = rim_in[:, place]
-                for block in range(block_count):
-                    state = state_in[:, place] * jnp.exp(-fade * (block * BLOCK))
-                    high = state.astype(bf16)
-                    low = (state - high.astype(f32)).astype(bf16)
-                    at = tile * 256 + block % 2 * 128
-                    carry_rows[block // 2, 0 : 3 * mode_count, at : at + 128] = jnp.concatenate(
-                        [high, low, high], 0
-                    )
+        else:
+            state_copy.wait_recv()
+
+        for tile in range(tile_count):
+            place = slice(tile * 128, (tile + 1) * 128)
+            fade = channel_decay(tile)
+            carry_rows[0, BLOCK : 2 * BLOCK, tile * 256 : tile * 256 + 128] = rim_in[:, place]
+            for block in range(block_count):
+                state = state_in[:, place] * jnp.exp(-fade * (block * BLOCK))
+                high = state.astype(bf16)
+                low = (state - high.astype(f32)).astype(bf16)
+                at = tile * 256 + block % 2 * 128
+                carry_rows[block // 2, 0 : 3 * mode_count, at : at + 128] = jnp.concatenate(
+                    [high, low, high], 0
+                )
 
     pair_spots = 2 * BLOCK // rows
     for pair in range(pair_count):
+        depth = (pair + 1) * 2 * BLOCK
+
+        def own_part(tile, carry):
+            place = pl.ds(pl.multiple_of(tile * 128, 128), 128)
+            columns = slice(block_count * BLOCK - depth, block_count * BLOCK)
+            source = jnp.concatenate(
+                [prod_all[0:depth, place], prod_all[BLOCK : BLOCK + depth, place]], 1
+            )
+            sums = grouped(toep, columns, source, tile * tile_groups * BLOCK)
+            for side in range(2):
+                at = (pair * 2 + side) * BLOCK
+                mixed_sum[at : at + BLOCK, place] = sums[side]
+            return carry
+
+        lax.fori_loop(0, tile_count, own_part, 0)
+
         if parts > 1:
 
             @pl.when(mine > 0)
             def _():
-                depth = 2 * BLOCK if pair == 0 else BLOCK
+                if pair == 0:
+                    take_carry()
+                reach = 2 * BLOCK if pair == 0 else BLOCK
 
                 def carried(tile, carry):
                     place = pl.ds(pl.multiple_of(tile * 128, 128), 128)
                     source = carry_rows[
-                        pair, 0:depth, pl.ds(pl.multiple_of(tile * 256, 256), 256)
+                        pair, 0:reach, pl.ds(pl.multiple_of(tile * 256, 256), 256)
                     ]
                     sums = grouped(
-                        carry_taps, slice(0, depth), source, tile * tile_groups * BLOCK
+                        carry_taps, slice(0, reach), source, tile * tile_groups * BLOCK
                     )
                     for side in range(2):
                         at = (pair * 2 + side) * BLOCK
@@ -704,14 +704,18 @@
     square_sum = jnp.sum(square, axis=1, keepdims=True)
     scale = 1.0 / jnp.sqrt(square_sum / (channels * tpn) + 1e-05)
 
-    def finish(chunk, carry):
-        start = pl.multiple_of(chunk * 256, 256)
-        gain = gain_ref[pl.ds(start, 256)].astype(f32).reshape(1, 256)
-        place = pl.ds(start, 256)
+    quarter = channels // 4
+    stores = []
+    for part_index in range(4):
+        place = slice(part_index * quarter, (part_index + 1) * quarter)
+        gain = gain_ref[place].astype(f32).reshape(1, quarter)
         out_ref[:, place] = (hidden[:, place] * gain * scale).astype(bf16)
-        return carry
-
-    lax.fori_loop(0, channels // 256, finish, 0)
+        stores.append(
+            pltpu.make_async_copy(
+                out_ref.at[:, place], out_hbm.at[:, place], store_sem.at[part_index]
+            )
+        )
+        stores[-1].start()
 
     @pl.when(me < n - 1)
     def _():
@@ -735,6 +739,8 @@
 
     for k in range(1, tpn):
         square_copy(k).wait_send()
+    for store in stores:
+        store.wait()
 
 
 def fused(part, n, tpn, *args):
@@ -752,8 +758,9 @@
         functools.partial(fused_kernel, part, n, tpn),
         out_shape=jax.ShapeDtypeStruct((rows, channels), bf16),
         in_specs=[pl.BlockSpec(memory_space=pltpu.HBM)] * 9,
-        out_specs=pl.BlockSpec(memory_space=pltpu.VMEM),
+        out_specs=pl.BlockSpec(memory_space=pltpu.HBM),
         scratch_shapes=[
+            pltpu.VMEM((rows, channels), bf16),
             pltpu.VMEM((rows, channels), bf16),
             pltpu.VMEM((rows, channels), bf16),
             pltpu.VMEM((rows, channels), bf16),
@@ -791,6 +798,7 @@
             pltpu.VMEM((rows, 128), f32),
             pltpu.VMEM((tpn, rows, 128), f32),
             dma((9,)),
+            dma((4,)),
             dma((2,)),
             dma((2,)),
             dma((part,)),
@@ -803,7 +811,7 @@
             dma((tpn,)),
         ],
         compiler_params=pltpu.CompilerParams(
-            collective_id=0, has_side_effects=True, vmem_limit_bytes=54200 * 1024
+            collective_id=0, has_side_effects=True, vmem_limit_bytes=63 * 1024 * 1024
         ),
     )(outer_input, inner_input, value_input, taps, medium, decay.T, residues.T, residual, gain)
 

time: 38.5 us -> 35.7 us (0.927)
  the two profiles are of different devices: /device:TPU:23 before, /device:TPU:31 now
where the time goes in v5:
time: 35.7 us; the launch traced here: 35.5 us
  Pallas kernels  33.6 us (94%)
  local copies, waits for them, and re-layouts  1.87 us (5%)
    pallas_call x1, Pallas kernels, fused(): pl.pallas_call(functools.partial(fused_kernel, part, n, tpn), out_shape=j...  33.6 us
    unnamed x1, local copies, waits for them, and re-layouts  1.87 us

profile of v5, /device:TPU:31, one launch (start us, length us, event | category | flops | bytes accessed | tf_op | source)
XLA Modules:
  0.0 35.5 jit_solution(190218901640186958)
XLA Ops:
  0.0 33.6 %shard_map.91 = bf16[64,4096]{1,0:T(8,128)(2,1)} custom-call(bf16[64,4096]{1,0:T(8,128)(2,1)} %outer_hbm.1, bf16[64,4096]{1,0:T(8,128)(2,1)} %inner_hbm.1, bf16[64,4096]{1,0:T(8,128)(2,1)} %value_hbm.1, bf16[3,7,4096]{2,1,0:T(8,128)(2,1)} %taps_hbm.1, bf16[128,256]{1,0:T(8,128)(2,1)} %medium_hbm.1, f32[16,256]{1,0:T(8,128)} %bitcast.2, f32[16,256]{1,0:T(8,128)} %bitcast.3, ...), custom_call_target="tpu_custom_call" | custom-call | tf_op jit(solution)/shard_map/pallas_call | solution.py:757
  33.7 1.9 %copy.11 = bf16[64,4096]{1,0:T(8,128)(2,1)} copy(bf16[64,4096]{1,0:T(8,128)(2,1)} %shard_map.91) | data formatting | bytes 1048576

commit v6 on v5

--- a/solution.py
+++ b/solution.py
@@ -303,17 +303,20 @@
 
     per_spot = width // step
 
-    def lower_product(chunk, carry):
-        start = pl.multiple_of(chunk * step, step)
-        inside = pl.ds(pl.multiple_of(lax.rem(chunk, per_spot) * step, step), step)
-        ext_a[8 : 8 + rows, :] = inner_ref[:, pl.ds(start, step)].astype(f32)
-        ext_b[8 : 8 + rows, :] = value_ref[:, pl.ds(start, step)].astype(f32)
-        inner_feat = windows(1, ext_a, start, step, 24, rows - 16)
-        value_feat = windows(2, ext_b, start, step, 24, rows - 16)
-        prod_out[chunk // per_spot, 16:rows, inside] = (inner_feat * value_feat).astype(bf16)
+    def lower_product(owner, carry):
+        for piece in range(per_spot):
+            low, high = ext_a.at[piece], ext_b.at[piece]
+            start = pl.multiple_of(owner * width + piece * step, step)
+            low[8 : 8 + rows, :] = inner_ref[:, pl.ds(start, step)].astype(f32)
+            high[8 : 8 + rows, :] = value_ref[:, pl.ds(start, step)].astype(f32)
+            inner_feat = windows(1, low, start, step, 24, rows - 16)
+            value_feat = windows(2, high, start, step, 24, rows - 16)
+            prod_out[owner, 16:rows, piece * step : (piece + 1) * step] = (
+                inner_feat * value_feat
+            ).astype(bf16)
         return carry
 
-    lax.fori_loop(0, channels // step, lower_product, 0, unroll=4)
+    lax.fori_loop(0, part, lower_product, 0)
 
     @pl.when(me > 0)
     def _():
@@ -321,14 +324,15 @@
 
     def upper_product(owner):
         for piece in range(per_spot):
+            low, high = ext_a.at[piece], ext_b.at[piece]
             start = pl.multiple_of(owner * width + piece * step, step)
             rim = halo_in[:, pl.ds(start, step)].astype(f32)
-            ext_a[0:8, :] = rim[0:8]
-            ext_b[0:8, :] = rim[8:16]
-            ext_a[8:24, :] = inner_ref[0:16, pl.ds(start, step)].astype(f32)
-            ext_b[8:24, :] = value_ref[0:16, pl.ds(start, step)].astype(f32)
-            inner_feat = windows(1, ext_a, start, step, 8, 16)
-            value_feat = windows(2, ext_b, start, step, 8, 16)
+            low[0:8, :] = rim[0:8]
+            high[0:8, :] = rim[8:16]
+            low[8:24, :] = inner_ref[0:16, pl.ds(start, step)].astype(f32)
+            high[8:24, :] = value_ref[0:16, pl.ds(start, step)].astype(f32)
+            inner_feat = windows(1, low, start, step, 8, 16)
+            value_feat = windows(2, high, start, step, 8, 16)
             prod_out[owner, 0:16, piece * step : (piece + 1) * step] = (
                 inner_feat * value_feat
             ).astype(bf16)
@@ -420,23 +424,7 @@
                 state_taps[1, place, :] = (value - high.astype(f32)).astype(bf16)
                 return carry
 
-            lax.fori_loop(0, group_count, decays, 0)
-
-    @pl.when(me > 0)
-    def _():
-        halo_copies[1].wait_recv()
-
-    def gate_chunk(chunk, carry):
-        start = pl.multiple_of(chunk * step, step)
-        low = start < half
-        rim_start = pl.multiple_of(lax.rem(start, half), step)
-        rim = gate_in[:, pl.ds(rim_start, step)].astype(f32)
-        ext_a[0:8, :] = jnp.where(low, rim[0:8], rim[8:16])
-        ext_a[8 : 8 + rows, :] = outer_ref[:, pl.ds(start, step)].astype(f32)
-        hidden[:, pl.ds(start, step)] = windows(0, ext_a, start, step, 8, rows)
-        return carry
-
-    lax.fori_loop(0, channels // step, gate_chunk, 0, unroll=4)
+            lax.fori_loop(0, group_count, decays, 0, unroll=4)
 
     def wait_product(place):
         @pl.when(spot != place)
@@ -653,6 +641,24 @@
             @pl.when(spot == place)
             def _():
                 mixed_in[place] = mixed_out[place]
+
+    @pl.when(me > 0)
+    def _():
+        halo_copies[1].wait_recv()
+
+    def gate_chunk(owner, carry):
+        low = owner * width < half
+        for piece in range(per_spot):
+            ext = ext_a.at[piece]
+            start = pl.multiple_of(owner * width + piece * step, step)
+            rim_start = pl.multiple_of(lax.rem(start, half), step)
+            rim = gate_in[:, pl.ds(rim_start, step)].astype(f32)
+            ext[0:8, :] = jnp.where(low, rim[0:8], rim[8:16])
+            ext[8 : 8 + rows, :] = outer_ref[:, pl.ds(start, step)].astype(f32)
+            hidden[:, pl.ds(start, step)] = windows(0, ext, start, step, 8, rows)
+        return carry
+
+    lax.fori_loop(0, part, gate_chunk, 0)
 
     loads[7].wait()
     loads[8].wait()
@@ -776,8 +782,8 @@
             pltpu.VMEM((16, channels), bf16),
             pltpu.VMEM((16, channels // 2), bf16),
             pltpu.VMEM((16, channels // 2), bf16),
-            pltpu.VMEM((rows + 8, step), f32),
-            pltpu.VMEM((rows + 8, step), f32),
+            pltpu.VMEM((width // step, rows + 8, step), f32),
+            pltpu.VMEM((width // step, rows + 8, step), f32),
             pltpu.VMEM((part, rows, width), bf16),
             pltpu.VMEM((BLOCK + tokens, width), bf16),
             pltpu.VMEM((2, all_groups, BLOCK), f32),

time: 35.7 us -> 35.7 us (level)
  no operation moved by 1% of the time
where the time goes in v6:
time: 35.7 us; the launch traced here: 35.5 us
  Pallas kernels  33.7 us (94%)
  local copies, waits for them, and re-layouts  1.87 us (5%)
    pallas_call x1, Pallas kernels, fused(): pl.pallas_call(functools.partial(fused_kernel, part, n, tpn), out_shape=j...  33.7 us
    unnamed x1, local copies, waits for them, and re-layouts  1.87 us

profile of v6, /device:TPU:31, one launch (start us, length us, event | category | flops | bytes accessed | tf_op | source)
XLA Modules:
  0.0 35.5 jit_solution(17178541089388218525)
XLA Ops:
  0.0 33.7 %shard_map.91 = bf16[64,4096]{1,0:T(8,128)(2,1)} custom-call(bf16[64,4096]{1,0:T(8,128)(2,1)} %outer_hbm.1, bf16[64,4096]{1,0:T(8,128)(2,1)} %inner_hbm.1, bf16[64,4096]{1,0:T(8,128)(2,1)} %value_hbm.1, bf16[3,7,4096]{2,1,0:T(8,128)(2,1)} %taps_hbm.1, bf16[128,256]{1,0:T(8,128)(2,1)} %medium_hbm.1, f32[16,256]{1,0:T(8,128)} %bitcast.2, f32[16,256]{1,0:T(8,128)} %bitcast.3, ...), custom_call_target="tpu_custom_call" | custom-call | tf_op jit(solution)/shard_map/pallas_call | solution.py:763
  33.7 1.9 %copy.11 = bf16[64,4096]{1,0:T(8,128)(2,1)} copy(bf16[64,4096]{1,0:T(8,128)(2,1)} %shard_map.91) | data formatting | bytes 1048576
